TPU v7x, 32 devices: a whole 2x2x4 slice. The times are simulated.
32 devices in a mesh: dp: 8 (over y, x, core), mp: 4 (over z).
Axes of the slice: x: 2, y: 2, z: 4, core: 2. Of those that a mesh axis runs over, the one named last changes fastest.
Arguments:
- tokens: bfloat16 [16384, 1024], P(('dp', 'mp')), may hold values from -6 to 6
- memory: bfloat16 [16384, 1024], P(('dp', 'mp')), may hold values from -6 to 6
- mem_lengths: int32 [16], P('dp'), may hold values from 256 to 1024, as said below
- cotangent: bfloat16 [16384, 1024], P(('dp', 'mp')), may hold values from -7.5 to 7.5
- attn_weights: float32 [8, 1024, 1024], P(None, 'dp', 'mp'), may hold values from -0.5 to 0.5
- ffn_weights: float32 [2, 1024, 4096], P(None, 'dp', 'mp'), may hold values from -0.25 to 0.25
- attn_momentum: float32 [8, 1024, 1024], P(None, 'dp', 'mp'), may hold values from -96 to 96
- ffn_momentum: float32 [2, 1024, 4096], P(None, 'dp', 'mp'), may hold values from -192 to 192
- norm_params: float32 [2, 3, 1024], replicated, may hold values from -0.8 to 1.3
- norm_first: float32 [2, 3, 1024], replicated, may hold values from -80 to 80
- norm_second: float32 [2, 3, 1024], replicated, may hold values from 16.384 to 65.536
Outputs:
- mixed_out: float32 [16384, 1024], P(('dp', 'mp'))
- input_grad: float32 [16384, 1024], P(('dp', 'mp'))
- memory_grad: float32 [16384, 1024], P(('dp', 'mp'))
- attn_weights_new: float32 [8, 1024, 1024], P(None, 'dp', 'mp')
- attn_momentum_new: float32 [8, 1024, 1024], P(None, 'dp', 'mp')
- ffn_weights_new: float32 [2, 1024, 4096], P(None, 'dp', 'mp')
- ffn_momentum_new: float32 [2, 1024, 4096], P(None, 'dp', 'mp')
- norm_grad_sums: float32 [2, 3, 1024], replicated
- norm_params_new: float32 [2, 3, 1024], replicated
- norm_first_new: float32 [2, 3, 1024], replicated
- norm_second_new: float32 [2, 3, 1024], replicated
Inputs may be any that keep to these rules, and one draw needn't show every extreme that they name: `mem_lengths`: each sequence's memory is valid at its first positions; one sequence has all 1024, one has 256.
All inputs are finite; a program needn't handle non-finite values.
Results may differ from a plain program's by a relative error of at most 0.015.
Values may be sent and summed in bfloat16 or wider, within the bound.
No kernel may reach another device: no remote copies, remote signals or barrier semaphores. Data moves between devices by JAX's collectives and lax.ppermute only.
A program may use at most 256 MiB of HBM per device.

v0:
```python
import jax
import jax.numpy as jnp
from jax import lax
from jax.sharding import PartitionSpec as P

D = 1024
HD = 64
MB = 128
NS = 5


highest = lax.Precision.HIGHEST
res_scale = 300.0**0.25
coef_one = 3.4445
coef_two = -4.775
coef_three = 2.0315
muon_rate = 0.3
adam_rate = 0.2
adam_count = 10.0


def gelu_exact(value):
    return 0.5 * value * (1.0 + lax.erf(value * 2.0 ** (-0.5)))


def gelu_slope(value):
    return 0.5 * (1.0 + lax.erf(value * 2.0 ** (-0.5))) + value * jnp.exp(-0.5 * value * value) * (
        2.0 * 3.141592653589793
    ) ** (-0.5)


def gather_rows(rows):
    return lax.all_gather(rows, "mp", axis=0, tiled=True)


def scatter_rows(partial_value):
    return lax.psum_scatter(partial_value, "mp", scatter_dimension=0, tiled=True)


def project(rows, weight):
    return jnp.dot(rows, weight, preferred_element_type=jnp.float32).astype(jnp.bfloat16)


def back_project(grads, weight):
    return jnp.einsum("tc,dc->td", grads, weight, preferred_element_type=jnp.float32)


def weight_grad(rows, grads):
    return jnp.einsum("td,tc->dc", rows, grads, preferred_element_type=jnp.float32)


def norm_forward(resid, gain, bias):
    row_mean = jnp.mean(resid, axis=-1, keepdims=True)
    centred = resid - row_mean
    variance = jnp.mean(centred * centred, axis=-1, keepdims=True)
    inv_std = lax.rsqrt(variance + 1e-05)
    normed = centred * inv_std
    return (normed * gain + bias, normed, inv_std)


def norm_backward(upstream, normed, inv_std, gain):
    scaled = upstream * gain
    centred = scaled - jnp.mean(scaled, axis=-1, keepdims=True)
    grad_resid = inv_std * (centred - normed * jnp.mean(scaled * normed, axis=-1, keepdims=True))
    return (grad_resid, jnp.sum(upstream * normed, axis=0), jnp.sum(upstream, axis=0))


def allowed_keys(query_count, key_count, length, causal):
    key_index = jnp.arange(key_count)[None, :]
    if causal:
        return jnp.arange(query_count)[:, None] >= key_index
    return jnp.broadcast_to(key_index < length, (query_count, key_count))


def attend_forward(queries, keys, values, lengths, causal):
    score_scale = queries.shape[-1] ** (-0.5)

    def per_sequence(inputs):
        query_rows, key_rows, value_rows, length = inputs
        allowed = allowed_keys(query_rows.shape[0], key_rows.shape[0], length, causal)
        scores = score_scale * jnp.einsum(
            "qhd,khd->hqk", query_rows, key_rows, preferred_element_type=jnp.float32
        )
        masked = jnp.where(allowed[None], scores, -1e30)
        row_max = jnp.max(masked, axis=-1, keepdims=True)
        lifted = jnp.exp(masked - row_max)
        row_total = jnp.sum(lifted, axis=-1, keepdims=True)
        attn_probs = (lifted / row_total).astype(jnp.bfloat16)
        context = jnp.einsum(
            "hqk,khd->qhd", attn_probs, value_rows, preferred_element_type=jnp.float32
        )
        return (context.astype(jnp.bfloat16), row_max + jnp.log(row_total))

    return lax.map(per_sequence, (queries, keys, values, lengths))


def attend_backward(queries, keys, values, lengths, log_totals, grad_ctx, causal):
    score_scale = queries.shape[-1] ** (-0.5)

    def per_sequence(inputs):
        query_rows, key_rows, value_rows, length, log_total, grad_rows = inputs
        allowed = allowed_keys(query_rows.shape[0], key_rows.shape[0], length, causal)
        scores = score_scale * jnp.einsum(
            "qhd,khd->hqk", query_rows, key_rows, preferred_element_type=jnp.float32
        )
        attn_probs = jnp.where(allowed[None], jnp.exp(scores - log_total), 0.0)
        grad_probs = jnp.einsum(
            "qhd,khd->hqk", grad_rows, value_rows, preferred_element_type=jnp.float32
        )
        grad_value = jnp.einsum(
            "hqk,qhd->khd",
            attn_probs.astype(jnp.bfloat16),
            grad_rows,
            preferred_element_type=jnp.float32,
        )
        row_inner = jnp.sum(attn_probs * grad_probs, axis=-1, keepdims=True)
        grad_scores = (attn_probs * (grad_probs - row_inner)).astype(jnp.bfloat16)
        grad_query = score_scale * jnp.einsum(
            "hqk,khd->qhd", grad_scores, key_rows, preferred_element_type=jnp.float32
        )
        grad_key = score_scale * jnp.einsum(
            "hqk,qhd->khd", grad_scores, query_rows, preferred_element_type=jnp.float32
        )
        return (
            grad_query.astype(jnp.bfloat16),
            grad_key.astype(jnp.bfloat16),
            grad_value.astype(jnp.bfloat16),
        )

    return lax.map(per_sequence, (queries, keys, values, lengths, log_totals, grad_ctx))


def muon_blocks(moment):
    slots, rows, cols = moment.shape
    return moment.reshape(slots, rows, cols // MB, MB)


def local_gram(blocks):
    return jnp.einsum(
        "sdbi,sdbj->sbij", blocks, blocks, precision=highest, preferred_element_type=jnp.float32
    )


def summed_grams(attn_blocks, ffn_blocks):
    return lax.psum((local_gram(attn_blocks), local_gram(ffn_blocks)), "dp")


def poly_step(blocks, gram):
    squared = jnp.einsum(
        "sbij,sbjk->sbik", gram, gram, precision=highest, preferred_element_type=jnp.float32
    )
    poly = coef_two * gram + coef_three * squared
    return coef_one * blocks + jnp.einsum(
        "sdbi,sbij->sdbj", blocks, poly, precision=highest, preferred_element_type=jnp.float32
    )


def rescale_first(blocks, gram):
    inverse = 1.0 / (jnp.sqrt(jnp.trace(gram, axis1=2, axis2=3)) + 1e-07)
    return (blocks * inverse[:, None, :, None], gram * (inverse * inverse)[:, :, None, None])


def on_device(
    tokens,
    memory,
    mem_lengths,
    cotangent,
    attn_weights,
    ffn_weights,
    attn_momentum,
    ffn_momentum,
    norm_params,
    norm_first,
    norm_second,
):
    attn_full, ffn_full = (
        lax.all_gather(attn_weights.astype(jnp.bfloat16), "dp", axis=1, tiled=True),
        lax.all_gather(ffn_weights.astype(jnp.bfloat16), "dp", axis=1, tiled=True),
    )
    token_rows, memory_rows = (
        lax.all_gather(tokens, "mp", axis=0, tiled=True),
        lax.all_gather(memory, "mp", axis=0, tiled=True),
    )
    seq_count = mem_lengths.shape[0]
    head_cols = attn_full.shape[2]
    local_heads = head_cols // HD

    def split_heads(rows):
        return rows.reshape(seq_count, -1, local_heads, HD)

    def merge_heads(arranged):
        return arranged.reshape(-1, head_cols)

    self_q = project(token_rows, attn_full[0])
    self_k = project(token_rows, attn_full[1])
    self_v = project(token_rows, attn_full[2])
    self_ctx, self_lse = attend_forward(
        split_heads(self_q), split_heads(self_k), split_heads(self_v), mem_lengths, True
    )
    self_flat = merge_heads(self_ctx)
    self_out = scatter_rows(back_project(self_flat, attn_full[3]))
    tokens_wide = tokens.astype(jnp.float32)
    first_out, normed_one, inv_one = norm_forward(
        res_scale * tokens_wide + self_out, norm_params[0, 0], norm_params[1, 0]
    )
    first_rows = gather_rows(first_out.astype(jnp.bfloat16))
    cross_q = project(first_rows, attn_full[4])
    cross_k = project(memory_rows, attn_full[5])
    cross_v = project(memory_rows, attn_full[6])
    cross_ctx, cross_lse = attend_forward(
        split_heads(cross_q), split_heads(cross_k), split_heads(cross_v), mem_lengths, False
    )
    cross_flat = merge_heads(cross_ctx)
    cross_out = scatter_rows(back_project(cross_flat, attn_full[7]))
    second, normed_two, inv_two = norm_forward(
        res_scale * first_out + cross_out, norm_params[0, 1], norm_params[1, 1]
    )
    second_rows = gather_rows(second.astype(jnp.bfloat16))
    hidden = jnp.dot(second_rows, ffn_full[0], preferred_element_type=jnp.float32)
    active = gelu_exact(hidden).astype(jnp.bfloat16)
    ffn_out = scatter_rows(back_project(active, ffn_full[1]))
    mixed_out, normed_three, inv_three = norm_forward(
        res_scale * second + ffn_out, norm_params[0, 2], norm_params[1, 2]
    )
    upstream = cotangent.astype(jnp.float32)
    grad_three, gain_three, bias_three = norm_backward(
        upstream, normed_three, inv_three, norm_params[0, 2]
    )
    grad_ffn_rows = gather_rows(grad_three.astype(jnp.bfloat16))
    grad_w_out = weight_grad(grad_ffn_rows, active)
    grad_active = jnp.dot(grad_ffn_rows, ffn_full[1], preferred_element_type=jnp.float32)
    grad_hidden = (grad_active * gelu_slope(hidden)).astype(jnp.bfloat16)
    grad_w_in = weight_grad(second_rows, grad_hidden)
    grad_second = res_scale * grad_three + scatter_rows(back_project(grad_hidden, ffn_full[0]))
    grad_two, gain_two, bias_two = norm_backward(
        grad_second, normed_two, inv_two, norm_params[0, 1]
    )
    grad_cross_rows = gather_rows(grad_two.astype(jnp.bfloat16))
    grad_cross_o = weight_grad(grad_cross_rows, cross_flat)
    grad_cross_ctx = jnp.dot(
        grad_cross_rows, attn_full[7], preferred_element_type=jnp.float32
    ).astype(jnp.bfloat16)
    grad_cq, grad_ck, grad_cv = attend_backward(
        split_heads(cross_q),
        split_heads(cross_k),
        split_heads(cross_v),
        mem_lengths,
        cross_lse,
        split_heads(grad_cross_ctx),
        False,
    )
    grad_cq = merge_heads(grad_cq)
    grad_ck = merge_heads(grad_ck)
    grad_cv = merge_heads(grad_cv)
    grad_cross_q = weight_grad(first_rows, grad_cq)
    grad_cross_k = weight_grad(memory_rows, grad_ck)
    grad_cross_v = weight_grad(memory_rows, grad_cv)
    back_first, memory_grad = (
        lax.psum_scatter(
            back_project(grad_cq, attn_full[4]), "mp", scatter_dimension=0, tiled=True
        ),
        lax.psum_scatter(
            back_project(grad_ck, attn_full[5]) + back_project(grad_cv, attn_full[6]),
            "mp",
            scatter_dimension=0,
            tiled=True,
        ),
    )
    grad_first = res_scale * grad_two + back_first
    grad_one, gain_one, bias_one = norm_backward(grad_first, normed_one, inv_one, norm_params[0, 0])
    grad_self_rows = gather_rows(grad_one.astype(jnp.bfloat16))
    grad_self_o = weight_grad(grad_self_rows, self_flat)
    grad_self_ctx = jnp.dot(
        grad_self_rows, attn_full[3], preferred_element_type=jnp.float32
    ).astype(jnp.bfloat16)
    grad_sq, grad_sk, grad_sv = attend_backward(
        split_heads(self_q),
        split_heads(self_k),
        split_heads(self_v),
        mem_lengths,
        self_lse,
        split_heads(grad_self_ctx),
        True,
    )
    grad_sq = merge_heads(grad_sq)
    grad_sk = merge_heads(grad_sk)
    grad_sv = merge_heads(grad_sv)
    grad_self_q = weight_grad(token_rows, grad_sq)
    grad_self_k = weight_grad(token_rows, grad_sk)
    grad_self_v = weight_grad(token_rows, grad_sv)
    back_tokens = (
        back_project(grad_sq, attn_full[0])
        + back_project(grad_sk, attn_full[1])
        + back_project(grad_sv, attn_full[2])
    )
    input_grad = res_scale * grad_one + scatter_rows(back_tokens)
    reduced = (
        lax.psum_scatter(grad_self_q, "dp", scatter_dimension=0, tiled=True),
        lax.psum_scatter(grad_self_k, "dp", scatter_dimension=0, tiled=True),
        lax.psum_scatter(grad_self_v, "dp", scatter_dimension=0, tiled=True),
        lax.psum_scatter(grad_self_o, "dp", scatter_dimension=0, tiled=True),
        lax.psum_scatter(grad_cross_q, "dp", scatter_dimension=0, tiled=True),
        lax.psum_scatter(grad_cross_k, "dp", scatter_dimension=0, tiled=True),
        lax.psum_scatter(grad_cross_v, "dp", scatter_dimension=0, tiled=True),
        lax.psum_scatter(grad_cross_o, "dp", scatter_dimension=0, tiled=True),
        lax.psum_scatter(grad_w_in, "dp", scatter_dimension=0, tiled=True),
        lax.psum_scatter(grad_w_out, "dp", scatter_dimension=0, tiled=True),
    )
    attn_reduced = jnp.stack(reduced[:8])
    ffn_reduced = jnp.stack(reduced[8:])
    local_norm = jnp.stack(
        [jnp.stack([gain_one, gain_two, gain_three]), jnp.stack([bias_one, bias_two, bias_three])]
    )
    norm_grad = lax.psum(local_norm, ("dp", "mp"))
    attn_momentum_new = 0.5 * attn_momentum + attn_reduced
    ffn_momentum_new = 0.5 * ffn_momentum + ffn_reduced
    attn_cur = muon_blocks(attn_momentum_new)
    ffn_cur = muon_blocks(ffn_momentum_new)
    for sweep_index in range(NS):
        gram_attn, gram_ffn = summed_grams(attn_cur, ffn_cur)
        if sweep_index == 0:
            attn_cur, gram_attn = rescale_first(attn_cur, gram_attn)
            ffn_cur, gram_ffn = rescale_first(ffn_cur, gram_ffn)
        attn_cur = poly_step(attn_cur, gram_attn)
        ffn_cur = poly_step(ffn_cur, gram_ffn)
    attn_orth = attn_cur.reshape(attn_weights.shape)
    ffn_orth = ffn_cur.reshape(ffn_weights.shape)
    step_scale = muon_rate * (D / MB) ** 0.5
    attn_weights_new = attn_weights - step_scale * attn_orth
    ffn_weights_new = ffn_weights - step_scale * ffn_orth
    norm_first_new = 0.9 * norm_first + 0.1 * norm_grad
    norm_second_new = 0.999 * norm_second + 0.001 * norm_grad * norm_grad
    step_size = (
        norm_first_new
        / (1.0 - 0.9**adam_count)
        / (jnp.sqrt(norm_second_new / (1.0 - 0.999**adam_count)) + 1e-08)
    )
    norm_params_new = norm_params - adam_rate * step_size
    return (
        mixed_out,
        input_grad,
        memory_grad,
        attn_weights_new,
        attn_momentum_new,
        ffn_weights_new,
        ffn_momentum_new,
        norm_grad,
        norm_params_new,
        norm_first_new,
        norm_second_new,
    )


def solution(mesh):
    return jax.shard_map(
        on_device,
        mesh=mesh,
        in_specs=(
            P(("dp", "mp"), None),
            P(("dp", "mp"), None),
            P("dp"),
            P(("dp", "mp"), None),
            P(None, "dp", "mp"),
            P(None, "dp", "mp"),
            P(None, "dp", "mp"),
            P(None, "dp", "mp"),
            P(),
            P(),
            P(),
        ),
        out_specs=(
            P(("dp", "mp"), None),
            P(("dp", "mp"), None),
            P(("dp", "mp"), None),
            P(None, "dp", "mp"),
            P(None, "dp", "mp"),
            P(None, "dp", "mp"),
            P(None, "dp", "mp"),
            P(),
            P(),
            P(),
            P(),
        ),
        check_vma=False,
    )
```

profile of v0, /device:TPU:0, one launch (start us, length us, event | category | flops | bytes accessed | tf_op | source)
XLA Modules:
  0.0 2764.7 jit_solution(8889684711299573431)
XLA Ops:
  10.1 83.0 %all-gather.10.cloned.1.call-done = bf16[2048,1024]{1,0:T(8,128)(2,1)} async-done(((bf16[512,1024]{1,0:T(8,128)(2,1)}), bf16[2048,1024]{1,0:T(8,128)(2,1)}) %all-gather.10.cloned.1.call-update) | async-done | bytes 4194320 | tf_op jit(solution)/shard_map/all_gather | solution.py:181
  192.5 143.3 %reduce-scatter.18.cloned.1.call-done = f32[512,1024]{1,0:T(8,128)} async-done(((f32[2048,1024]{1,0:T(8,128)}), f32[512,1024]{1,0:T(8,128)}) %reduce-scatter.18.cloned.1.call-update) | async-done | bytes 2097168 | tf_op jit(solution)/shard_map/reduce_scatter | solution.py:37
  340.5 78.2 %all-gather.14.cloned.1.call-done = bf16[2048,1024]{1,0:T(8,128)(2,1)} async-done(((bf16[512,1024]{1,0:T(8,128)(2,1)}), bf16[2048,1024]{1,0:T(8,128)(2,1)}) %all-gather.14.cloned.1.call-update) | async-done | bytes 4194320 | tf_op jit(solution)/shard_map/all_gather | solution.py:182
  436.9 63.2 %all-gather.16.cloned.1.call-done = bf16[2048,1024]{1,0:T(8,128)(2,1)} async-done(((bf16[512,1024]{1,0:T(8,128)(2,1)}), bf16[2048,1024]{1,0:T(8,128)(2,1)}) %all-gather.16.cloned.1.call-update) | async-done | bytes 4194320 | tf_op jit(solution)/shard_map/all_gather | solution.py:33
  549.1 140.7 %reduce-scatter.20.cloned.1.call-done = f32[512,1024]{1,0:T(8,128)} async-done(((f32[2048,1024]{1,0:T(8,128)}), f32[512,1024]{1,0:T(8,128)}) %reduce-scatter.20.cloned.1.call-update) | async-done | bytes 2097168 | tf_op jit(solution)/shard_map/reduce_scatter | solution.py:37
  729.8 82.9 %all-gather.18.cloned.1.call-done = bf16[2048,1024]{1,0:T(8,128)(2,1)} async-done(((bf16[512,1024]{1,0:T(8,128)(2,1)}), bf16[2048,1024]{1,0:T(8,128)(2,1)}) %all-gather.18.cloned.1.call-update) | async-done | bytes 4194320 | tf_op jit(solution)/shard_map/all_gather | solution.py:33
  831.5 143.1 %reduce-scatter.22.cloned.1.call-done = f32[512,1024]{1,0:T(8,128)} async-done(((f32[2048,1024]{1,0:T(8,128)}), f32[512,1024]{1,0:T(8,128)}) %reduce-scatter.22.cloned.1.call-update) | async-done | bytes 2097168 | tf_op jit(solution)/shard_map/reduce_scatter | solution.py:37
  983.3 81.4 %all-gather.22.cloned.1.call-done = bf16[2048,1024]{1,0:T(8,128)(2,1)} async-done(((bf16[512,1024]{1,0:T(8,128)(2,1)}), bf16[2048,1024]{1,0:T(8,128)(2,1)}) %all-gather.22.cloned.1.call-update) | async-done | bytes 4194320 | tf_op jit(solution)/shard_map/all_gather | solution.py:33
  1083.8 143.1 %reduce-scatter.24.cloned.1.call-done = f32[512,1024]{1,0:T(8,128)} async-done(((f32[2048,1024]{1,0:T(8,128)}), f32[512,1024]{1,0:T(8,128)}) %reduce-scatter.24.cloned.1.call-update) | async-done | bytes 2097168 | tf_op jit(solution)/shard_map/reduce_scatter | solution.py:37
  1235.1 81.6 %all-gather.24.cloned.1.call-done = bf16[2048,1024]{1,0:T(8,128)(2,1)} async-done(((bf16[512,1024]{1,0:T(8,128)(2,1)}), bf16[2048,1024]{1,0:T(8,128)(2,1)}) %all-gather.24.cloned.1.call-update) | async-done | bytes 4194320 | tf_op jit(solution)/shard_map/all_gather | solution.py:33
  1333.1 88.7 %while.54 = (s32[]{:T(128)}, bf16[2,1024,4,64]{1,3,2,0:T(8,128)(2,1)}, bf16[2,1024,4,64]{1,3,2,0:T(8,128)(2,1)}, bf16[2,1024,4,64]{1,3,2,0:T(8,128)(2,1)}, bf16[...) while((s32[]{:T(128)}, ...), condition=%wide.region_24.25_spmd, body=%wide.region_22.24_spmd.sunk | while | flops 2723410944 | bytes 173104368 | solution.py:130
  1431.1 143.1 %reduce-scatter.26.cloned.1.call-done = f32[512,1024]{1,0:T(8,128)} async-done(((f32[2048,1024]{1,0:T(8,128)}), f32[512,1024]{1,0:T(8,128)}) %reduce-scatter.26.cloned.1.call-update) | async-done | bytes 2097168 | tf_op jit(solution)/shard_map/reduce_scatter | solution.py:259
  1600.9 61.1 %all-gather.26.cloned.1.call-done = bf16[2048,1024]{1,0:T(8,128)(2,1)} async-done(((bf16[512,1024]{1,0:T(8,128)(2,1)}), bf16[2048,1024]{1,0:T(8,128)(2,1)}) %all-gather.26.cloned.1.call-update) | async-done | bytes 4194320 | tf_op jit(solution)/shard_map/all_gather | solution.py:33
  1671.4 97.7 %while.55 = (s32[]{:T(128)}, bf16[2,1024,4,64]{1,3,2,0:T(8,128)(2,1)}, bf16[2,1024,4,64]{1,3,2,0:T(8,128)(2,1)}, bf16[2,1024,4,64]{1,3,2,0:T(8,128)(2,1)}, bf16[...) while((s32[]{:T(128)}, ...), condition=%wide.region_30.31_spmd, body=%wide.region_28.30_spmd.sunk | while | flops 2724458496 | bytes 191976800 | solution.py:130
  1850.5 38.3 %reduce-scatter.36.cloned.1.call-done = f32[128,256]{0,1:T(8,128)} async-done(((f32[1024,256]{0,1:T(8,128)}), f32[128,256]{0,1:T(8,128)}) %reduce-scatter.36.cloned.1.call-update) | async-done | bytes 131088 | tf_op jit(solution)/shard_map/reduce_scatter | solution.py:300
  1928.8 38.3 %reduce-scatter.40.cloned.1.call-done = f32[128,256]{0,1:T(8,128)} async-done(((f32[1024,256]{0,1:T(8,128)}), f32[128,256]{0,1:T(8,128)}) %reduce-scatter.40.cloned.1.call-update) | async-done | bytes 131088 | tf_op jit(solution)/shard_map/reduce_scatter | solution.py:302
  2007.2 38.3 %reduce-scatter.44.cloned.1.call-done = f32[128,256]{0,1:T(8,128)} async-done(((f32[1024,256]{0,1:T(8,128)}), f32[128,256]{0,1:T(8,128)}) %reduce-scatter.44.cloned.1.call-update) | async-done | bytes 131088 | tf_op jit(solution)/shard_map/reduce_scatter | solution.py:304
  2090.6 61.2 %all-reduce.19.cloned.1.call-done = (f32[8,2,128,128]{3,2,1,0:T(8,128)}, f32[2,8,128,128]{3,2,1,0:T(8,128)}) async-done(((f32[8,2,128,128]{3,2,1,0:T(8,128)}, f32[2,8,128,128]{3,2,1,0:T(8,128)}), (f32[8,2,128,128]{3,2,1,0:T(8,128)}, f32[2,8,128,128]{3,2,1,0:T(8,128)})) %all-reduce.19.cloned.1.call-update) | async-done | bytes 2097168 | tf_op jit(solution)/shard_map/psum | solution.py:145
  2170.4 60.7 %all-reduce.17.cloned.1.call-done = (f32[8,2,128,128]{3,2,1,0:T(8,128)}, f32[2,8,128,128]{3,2,1,0:T(8,128)}) async-done(((f32[8,2,128,128]{3,2,1,0:T(8,128)}, f32[2,8,128,128]{3,2,1,0:T(8,128)}), (f32[8,2,128,128]{3,2,1,0:T(8,128)}, f32[2,8,128,128]{3,2,1,0:T(8,128)})) %all-reduce.17.cloned.1.call-update) | async-done | bytes 2097168 | tf_op jit(solution)/shard_map/psum | solution.py:145
  2249.0 60.7 %all-reduce.15.cloned.1.call-done = (f32[8,2,128,128]{3,2,1,0:T(8,128)}, f32[2,8,128,128]{3,2,1,0:T(8,128)}) async-done(((f32[8,2,128,128]{3,2,1,0:T(8,128)}, f32[2,8,128,128]{3,2,1,0:T(8,128)}), (f32[8,2,128,128]{3,2,1,0:T(8,128)}, f32[2,8,128,128]{3,2,1,0:T(8,128)})) %all-reduce.15.cloned.1.call-update) | async-done | bytes 2097168 | tf_op jit(solution)/shard_map/psum | solution.py:145
  2332.0 54.8 %all-reduce.13.cloned.1.call-done = (f32[8,2,128,128]{3,2,1,0:T(8,128)}, f32[2,8,128,128]{3,2,1,0:T(8,128)}) async-done(((f32[8,2,128,128]{3,2,1,0:T(8,128)}, f32[2,8,128,128]{3,2,1,0:T(8,128)}), (f32[8,2,128,128]{3,2,1,0:T(8,128)}, f32[2,8,128,128]{3,2,1,0:T(8,128)})) %all-reduce.13.cloned.1.call-update) | async-done | bytes 2097168 | tf_op jit(solution)/shard_map/psum | solution.py:145
  2423.1 39.7 %psum.87 = f32[2,3,1024]{2,1,0:T(4,128)S(1)} all-reduce(f32[2,3,1024]{2,1,0:T(4,128)S(1)} %pad_maximum_fusion), channel_id=1, replica_groups=mesh['dp'=8,'mp'=4] {'dp','mp'}, use_global_device_ids=true, to_apply=%region_61.62 | all-reduce | flops 6144 | bytes 49152 | tf_op jit(solution)/shard_map/psum | solution.py:314
  2485.3 124.3 %reduce-scatter.28.cloned.1.call-done = f32[512,1024]{1,0:T(8,128)} async-done(((f32[2048,1024]{1,0:T(8,128)}), f32[512,1024]{1,0:T(8,128)}) %reduce-scatter.28.cloned.1.call-update) | async-done | bytes 2097168 | tf_op jit(solution)/shard_map/reduce_scatter | solution.py:37
  2612.9 144.8 %reduce-scatter.30.cloned.1.call-done = f32[512,1024]{1,0:T(8,128)} async-done(((f32[2048,1024]{1,0:T(8,128)}), f32[512,1024]{1,0:T(8,128)}) %reduce-scatter.30.cloned.1.call-update) | async-done | bytes 2097168 | tf_op jit(solution)/shard_map/reduce_scatter | solution.py:262
  (509 shorter events, 895.4 us)
Async XLA Ops:
  10.1 325.8 %reduce-scatter.18.cloned.1.call-start = ((), (), s32[]{:S(2)}) async-start(), calls=%async_computation.19 | async-start | bytes 10485760 | tf_op jit(solution)/shard_map/reduce_scatter | solution.py:37
  191.2 227.6 %all-gather.14.cloned.1.call-start = ((), (), s32[]{:S(2)}) async-start(), calls=%async_computation.20 | async-start | bytes 5242880 | tf_op jit(solution)/shard_map/all_gather | solution.py:182
  191.8 308.3 %all-gather.16.cloned.1.call-start = ((), (), s32[]{:S(2)}) async-start(), calls=%async_computation.21 | async-start | bytes 5242880 | tf_op jit(solution)/shard_map/all_gather | solution.py:33
  340.5 349.3 %reduce-scatter.20.cloned.1.call-start = ((), (), s32[]{:S(2)}) async-start(), calls=%async_computation.22 | async-start | bytes 10485760 | tf_op jit(solution)/shard_map/reduce_scatter | solution.py:37
  546.6 183.1 %all-gather.20.cloned.1.call-start = ((), (), s32[]{:S(2)}) async-start(), calls=%async_computation.24 | async-start | bytes 4718592 | tf_op jit(solution)/shard_map/all_gather | solution.py:178
  548.8 263.9 %all-gather.18.cloned.1.call-start = ((), (), s32[]{:S(2)}) async-start(), calls=%async_computation.23 | async-start | bytes 5242880 | tf_op jit(solution)/shard_map/all_gather | solution.py:33
  695.5 279.1 %reduce-scatter.22.cloned.1.call-start = ((), (), s32[]{:S(2)}) async-start(), calls=%async_computation.25 | async-start | bytes 10485760 | tf_op jit(solution)/shard_map/reduce_scatter | solution.py:37
  831.4 233.3 %all-gather.22.cloned.1.call-start = ((), (), s32[]{:S(2)}) async-start(), calls=%async_computation.26 | async-start | bytes 5242880 | tf_op jit(solution)/shard_map/all_gather | solution.py:33
  983.0 243.9 %reduce-scatter.24.cloned.1.call-start = ((), (), s32[]{:S(2)}) async-start(), calls=%async_computation.27 | async-start | bytes 10485760 | tf_op jit(solution)/shard_map/reduce_scatter | solution.py:37
  1083.8 232.9 %all-gather.24.cloned.1.call-start = ((), (), s32[]{:S(2)}) async-start(), calls=%async_computation.28 | async-start | bytes 5242880 | tf_op jit(solution)/shard_map/all_gather | solution.py:33
  1235.1 339.2 %reduce-scatter.26.cloned.1.call-start = ((), (), s32[]{:S(2)}) async-start(), calls=%async_computation.29 | async-start | bytes 10485760 | tf_op jit(solution)/shard_map/reduce_scatter | solution.py:259
  1431.1 230.9 %all-gather.26.cloned.1.call-start = ((), (), s32[]{:S(2)}) async-start(), calls=%async_computation.30 | async-start | bytes 5242880 | tf_op jit(solution)/shard_map/all_gather | solution.py:33
  1580.4 224.7 %reduce-scatter.48.cloned.1.call-start = ((), (), s32[]{:S(2)}) async-start(), calls=%async_computation.41 | async-start | bytes 4718592 | tf_op jit(solution)/shard_map/reduce_scatter | solution.py:306
  1590.5 214.5 %reduce-scatter.50.cloned.1.call-start = ((), (), s32[]{:S(2)}) async-start(), calls=%async_computation.42 | async-start | bytes 4718592 | tf_op jit(solution)/shard_map/reduce_scatter | solution.py:307
  1600.9 213.9 %reduce-scatter.32.cloned.1.call-start = ((), (), s32[]{:S(2)}) async-start(), calls=%async_computation.33 | async-start | bytes 1179648 | tf_op jit(solution)/shard_map/reduce_scatter | solution.py:298
  1784.7 143.2 %reduce-scatter.38.cloned.1.call-start = ((), (), s32[]{:S(2)}) async-start(), calls=%async_computation.36 | async-start | bytes 1179648 | tf_op jit(solution)/shard_map/reduce_scatter | solution.py:301
  1789.4 177.8 %reduce-scatter.40.cloned.1.call-start = ((), (), s32[]{:S(2)}) async-start(), calls=%async_computation.37 | async-start | bytes 1179648 | tf_op jit(solution)/shard_map/reduce_scatter | solution.py:302
  1793.9 212.4 %reduce-scatter.42.cloned.1.call-start = ((), (), s32[]{:S(2)}) async-start(), calls=%async_computation.38 | async-start | bytes 1179648 | tf_op jit(solution)/shard_map/reduce_scatter | solution.py:303
  1798.7 246.9 %reduce-scatter.44.cloned.1.call-start = ((), (), s32[]{:S(2)}) async-start(), calls=%async_computation.39 | async-start | bytes 1179648 | tf_op jit(solution)/shard_map/reduce_scatter | solution.py:304
  1803.6 281.0 %reduce-scatter.46.cloned.1.call-start = ((), (), s32[]{:S(2)}) async-start(), calls=%async_computation.40 | async-start | bytes 1179648 | tf_op jit(solution)/shard_map/reduce_scatter | solution.py:305
  1814.7 337.2 %all-reduce.19.cloned.1.call-start = ((), (), s32[]{:S(2)}) async-start(), calls=%async_computation.47 | async-start | bytes 4194304 | tf_op jit(solution)/shard_map/psum | solution.py:145
  2090.2 140.9 %all-reduce.17.cloned.1.call-start = ((), (), s32[]{:S(2)}) async-start(), calls=%async_computation.46 | async-start | bytes 4194304 | tf_op jit(solution)/shard_map/psum | solution.py:145
  2401.9 207.7 %reduce-scatter.28.cloned.1.call-start = ((), (), s32[]{:S(2)}) async-start(), calls=%async_computation.31 | async-start | bytes 10485760 | tf_op jit(solution)/shard_map/reduce_scatter | solution.py:37
  2413.7 344.0 %reduce-scatter.30.cloned.1.call-start = ((), (), s32[]{:S(2)}) async-start(), calls=%async_computation.32 | async-start | bytes 10485760 | tf_op jit(solution)/shard_map/reduce_scatter | solution.py:262
  (116 other events, 3595.6 us)
Sparse Core Ops, SparseCore 0:
  9.6 83.4 all-gather.9
  191.3 144.4 reduce-scatter.17
  337.2 81.4 all-gather.13
  420.8 79.2 all-gather.15
  546.8 142.9 reduce-scatter.19
  692.3 37.4 all-gather.19
  731.9 80.7 all-gather.17
  831.5 142.9 reduce-scatter.21
  983.1 81.4 all-gather.21
  1083.9 142.9 reduce-scatter.23
  1235.2 81.4 all-gather.23
  1431.2 143.0 reduce-scatter.25
  1580.5 81.4 all-gather.25
  1665.2 49.8 reduce-scatter.47
  1718.7 51.3 reduce-scatter.49
  1852.8 35.9 reduce-scatter.35
  1931.0 36.0 reduce-scatter.39
  2090.3 61.4 all-reduce.18
  2170.3 60.7 all-reduce.16
  2248.9 60.7 all-reduce.14
  2326.0 60.7 all-reduce.12
  2402.0 61.1 all-reduce.10
  2465.4 144.1 reduce-scatter.27
  2612.5 145.1 reduce-scatter.29
  (7 shorter events, 250.0 us)
where the time goes:
time: 2770 us; the launch traced here: 2760 us
  waiting for transfers between devices  2090 us (75%)
  matrix products  397 us (14%)
  other arithmetic  111 us (4%)
  local copies, waits for them, and re-layouts  108 us (4%)
  blocking collectives  39.7 us (1%)
    reduce_scatter x5, waiting for transfers between devices, scatter_rows(): lax.psum_scatter(partial_value, 'mp', scatter_dimension=0, tiled=True)  694 us
    all_gather x5, waiting for transfers between devices, gather_rows(): return lax.all_gather(rows, 'mp', axis=0, tiled=True)  370 us
    psum x5, waiting for transfers between devices, summed_grams(): return lax.psum((local_gram(attn_blocks), local_gram(ffn_blocks)), 'dp')  237 us
    reduce_scatter x1, waiting for transfers between devices, on_device(): lax.psum_scatter(back_project(grad_ck, attn_full[5]) + back_project(grad_...  145 us
    reduce_scatter x1, waiting for transfers between devices, on_device(): lax.psum_scatter(back_project(grad_cq, attn_full[4]), 'mp', scatter_dimen...  143 us
    all_gather x1, waiting for transfers between devices, on_device(): lax.all_gather(tokens, 'mp', axis=0, tiled=True)  83 us
    all_gather x1, waiting for transfers between devices, on_device(): lax.all_gather(memory, 'mp', axis=0, tiled=True)  78.2 us
    dot_general x10, matrix products, back_project(): jnp.einsum('tc,dc->td', grads, weight, preferred_element_type=jnp.float32)  56.8 us
  transfers between devices with their start and end apart: 31, of which 27 were waited for; matrix products, arithmetic and copies ran while one was open for 9% of the time, Pallas kernels for 0%

commit v1 on v0

v1 whole, which is shorter than its diff:
```python
import functools

import jax
import jax.numpy as jnp
from jax import lax
from jax.experimental import pallas as pl
from jax.experimental.pallas import tpu as pltpu
from jax.sharding import Mesh, PartitionSpec as P

HD = 64
MB = 128
NS = 5
PAIR = 2 * HD
QCHUNK = 256
highest = lax.Precision.HIGHEST
res_scale = 300.0**0.25
coef_one = 3.4445
coef_two = -4.775
coef_three = 2.0315
muon_rate = 0.3
adam_rate = 0.2
adam_count = 10.0
score_scale = HD ** (-0.5)
f32 = jnp.float32
bf16 = jnp.bfloat16


def gelu_exact(value):
    return 0.5 * value * (1.0 + lax.erf(value * 2.0 ** (-0.5)))


def gelu_slope(value):
    return 0.5 * (1.0 + lax.erf(value * 2.0 ** (-0.5))) + value * jnp.exp(-0.5 * value * value) * (
        2.0 * 3.141592653589793
    ) ** (-0.5)


def norm_forward(resid, gain, bias):
    row_mean = jnp.mean(resid, axis=-1, keepdims=True)
    centred = resid - row_mean
    variance = jnp.mean(centred * centred, axis=-1, keepdims=True)
    inv_std = lax.rsqrt(variance + 1e-05)
    normed = centred * inv_std
    return (normed * gain + bias, normed, inv_std)


def norm_backward(upstream, normed, inv_std, gain):
    scaled = upstream * gain
    centred = scaled - jnp.mean(scaled, axis=-1, keepdims=True)
    grad_resid = inv_std * (centred - normed * jnp.mean(scaled * normed, axis=-1, keepdims=True))
    return (grad_resid, jnp.sum(upstream * normed, axis=0), jnp.sum(upstream, axis=0))


def nt_dot(left, right):
    return lax.dot_general(left, right, (((1,), (1,)), ((), ())), preferred_element_type=f32)


def nn_dot(left, right):
    return lax.dot_general(left, right, (((1,), (0,)), ((), ())), preferred_element_type=f32)


def flip(value):
    return jnp.transpose(value).astype(bf16)


def only_head(value, head):
    lane = lax.broadcasted_iota(jnp.int32, value.shape, 1)
    keep = (lane < HD) if head == 0 else (lane >= HD)
    return jnp.where(keep, value, 0.0).astype(bf16)


def in_place_order(ref, slot, shift):
    half = ref.shape[-2] // 2
    low = ref[slot, pl.ds(pl.multiple_of(shift, half), half), :]
    high = ref[slot, pl.ds(pl.multiple_of(half - shift, half), half), :]
    return jnp.concatenate([low.astype(f32), high.astype(f32)], axis=0)


def row_of(start, shift, count, chunk, causal):
    if not causal:
        return pl.ds(start, chunk)
    row = start + shift
    row = jnp.where(row >= count, row - count, row)
    return pl.ds(pl.multiple_of(row, chunk), chunk)


def key_span(causal, start, size, key_count):
    return min(start + size, key_count) if causal else key_count


def scores_by_key(keys, queries, start, length, causal):
    scores = nt_dot(keys, queries)
    key_at = lax.broadcasted_iota(jnp.int32, scores.shape, 0)
    if causal:
        query_at = start + lax.broadcasted_iota(jnp.int32, scores.shape, 1)
        return jnp.where(key_at <= query_at, scores, -1e30)
    return jnp.where(key_at < length, scores, -1e30)


def forward_kernel(causal, chunk, at_ref, q_ref, k_ref, v_ref, ctx_ref, lse_ref):
    queries, key_count = q_ref.shape[-2], k_ref.shape[-2]
    length, shift = at_ref[0], at_ref[1]
    keys = in_place_order(k_ref, 0, shift) * score_scale
    values_t = flip(in_place_order(v_ref, 0, shift))
    scaled = [only_head(keys, head) for head in (0, 1)]
    for start in range(0, queries, chunk):
        span = key_span(causal, start, chunk, key_count)
        rows = row_of(start, shift, queries, chunk, causal)
        query_rows = q_ref[0, rows, :]
        parts = []
        for head in (0, 1):
            scores = scores_by_key(scaled[head][:span], query_rows, start, length, causal)
            top = jnp.max(scores, axis=0, keepdims=True)
            lifted = jnp.exp(scores - top)
            total = jnp.sum(lifted, axis=0, keepdims=True)
            mixed = nn_dot(values_t[head * HD : (head + 1) * HD, :span], lifted.astype(bf16))
            parts.append(mixed / total)
            lse_ref[0, head : head + 1, start : start + chunk] = top + jnp.log(total)
        both = jnp.concatenate(parts, axis=0)
        ctx_ref[rows, :] = jnp.transpose(both).astype(bf16)


def backward_kernel(
    causal, chunk, at_ref, q_ref, k_ref, v_ref, ctx_ref, grad_ref, lse_ref,
    gq_ref, gkv_ref, gk_acc, gv_acc,
):
    queries, key_count = q_ref.shape[-2], k_ref.shape[-2]
    length, shift = at_ref[0], at_ref[1]
    keys = in_place_order(k_ref, 0, shift) * score_scale
    values = in_place_order(v_ref, 0, shift)
    scaled = [only_head(keys, head) for head in (0, 1)]
    lane_values = [only_head(values, head) for head in (0, 1)]
    scaled_t = flip(keys)
    gk_acc[...] = jnp.zeros_like(gk_acc)
    gv_acc[...] = jnp.zeros_like(gv_acc)
    for start in range(0, queries, chunk):
        span = key_span(causal, start, chunk, key_count)
        rows = row_of(start, shift, queries, chunk, causal)
        query_rows = q_ref[0, rows, :]
        grad_rows = grad_ref[rows, :]
        query_wide, grad_wide = query_rows.astype(f32), grad_rows.astype(f32)
        inner = jnp.transpose(grad_wide * ctx_ref[rows, :].astype(f32))
        parts = []
        for head in (0, 1):
            scores = scores_by_key(scaled[head][:span], query_rows, start, length, causal)
            probs = jnp.exp(scores - lse_ref[0, head : head + 1, start : start + chunk])
            grad_probs = nt_dot(lane_values[head][:span], grad_rows)
            delta = jnp.sum(inner[head * HD : (head + 1) * HD], axis=0, keepdims=True)
            grad_scores = (probs * (grad_probs - delta)).astype(bf16)
            gv_acc[:span, :] += nn_dot(probs.astype(bf16), only_head(grad_wide, head))
            gk_acc[:span, :] += nn_dot(grad_scores, only_head(query_wide, head))
            parts.append(nn_dot(scaled_t[head * HD : (head + 1) * HD, :span], grad_scores))
        gq_ref[rows, :] = jnp.transpose(jnp.concatenate(parts, axis=0)).astype(bf16)
    half = key_count // 2
    low = pl.ds(pl.multiple_of(shift, half), half)
    high = pl.ds(pl.multiple_of(half - shift, half), half)
    gkv_ref[0, low, :] = (gk_acc[:half, :] * score_scale).astype(bf16)
    gkv_ref[0, high, :] = (gk_acc[half:, :] * score_scale).astype(bf16)
    gkv_ref[1, low, :] = gv_acc[:half, :].astype(bf16)
    gkv_ref[1, high, :] = gv_acc[half:, :].astype(bf16)


def source_block(rows, slot):
    return pl.BlockSpec((1, rows, PAIR), lambda pair, at: (slot, 0, pair))


def attend_forward(query_src, key_src, value_src, at, causal):
    queries, cols = query_src[0].shape[1:]
    key_count = key_src[0].shape[1]
    chunk = min(QCHUNK, queries // 2)
    work = queries * key_count * cols
    return pl.pallas_call(
        functools.partial(forward_kernel, causal, chunk),
        grid_spec=pltpu.PrefetchScalarGridSpec(
            num_scalar_prefetch=1,
            grid=(cols // PAIR,),
            in_specs=[
                source_block(queries, query_src[1]),
                source_block(key_count, key_src[1]),
                source_block(key_count, value_src[1]),
            ],
            out_specs=[
                pl.BlockSpec((queries, PAIR), lambda pair, at: (0, pair)),
                pl.BlockSpec((1, 8, queries), lambda pair, at: (pair, 0, 0)),
            ],
        ),
        out_shape=[
            jax.ShapeDtypeStruct((queries, cols), bf16),
            jax.ShapeDtypeStruct((cols // PAIR, 8, queries), f32),
        ],
        compiler_params=pltpu.CompilerParams(vmem_limit_bytes=48 * 2**20),
        cost_estimate=pl.CostEstimate(
            flops=32 * work, bytes_accessed=8 * queries * cols, transcendentals=work // HD
        ),
        name="attend_forward_causal" if causal else "attend_forward_cross",
    )(at, query_src[0], key_src[0], value_src[0])


def attend_backward(query_src, key_src, value_src, at, ctx, grad_ctx, lse, causal):
    queries, cols = query_src[0].shape[1:]
    key_count = key_src[0].shape[1]
    chunk = min(QCHUNK, queries // 2)
    flat = pl.BlockSpec((queries, PAIR), lambda pair, at: (0, pair))
    work = queries * key_count * cols
    return pl.pallas_call(
        functools.partial(backward_kernel, causal, chunk),
        grid_spec=pltpu.PrefetchScalarGridSpec(
            num_scalar_prefetch=1,
            grid=(cols // PAIR,),
            in_specs=[
                source_block(queries, query_src[1]),
                source_block(key_count, key_src[1]),
                source_block(key_count, value_src[1]),
                flat,
                flat,
                pl.BlockSpec((1, 8, queries), lambda pair, at: (pair, 0, 0)),
            ],
            out_specs=[flat, pl.BlockSpec((2, key_count, PAIR), lambda pair, at: (0, 0, pair))],
            scratch_shapes=[pltpu.VMEM((key_count, PAIR), f32), pltpu.VMEM((key_count, PAIR), f32)],
        ),
        out_shape=[
            jax.ShapeDtypeStruct((queries, cols), bf16),
            jax.ShapeDtypeStruct((2, key_count, cols), bf16),
        ],
        compiler_params=pltpu.CompilerParams(vmem_limit_bytes=48 * 2**20),
        cost_estimate=pl.CostEstimate(
            flops=40 * work, bytes_accessed=16 * queries * cols, transcendentals=work // HD
        ),
        name="attend_backward_causal" if causal else "attend_backward_cross",
    )(at, query_src[0], key_src[0], value_src[0], ctx, grad_ctx, lse)


def assemble_kernel(at_ref, own_ref, inner_ref, outer_ref, far_low_ref, far_high_ref, out_ref):
    which = pl.program_id(1) ^ at_ref[0]
    half = far_low_ref.shape[1]

    for code, ref in ((0, own_ref), (1, inner_ref), (2, outer_ref)):
        @pl.when(which == code)
        def _(ref=ref):
            out_ref[...] = ref[...]

    @pl.when(which == 3)
    def _():
        out_ref[:, :half, :] = far_low_ref[...]
        out_ref[:, half:, :] = far_high_ref[...]


def assemble(position, own, inner, outer, far_low, far_high):
    slots, rows, cols = own.shape
    whole = pl.BlockSpec((1, rows, cols), lambda slot, block, at: (slot, 0, 0))
    half = pl.BlockSpec((1, rows // 2, cols), lambda slot, block, at: (slot, 0, 0))
    return pl.pallas_call(
        assemble_kernel,
        grid_spec=pltpu.PrefetchScalarGridSpec(
            num_scalar_prefetch=1,
            grid=(slots, 4),
            in_specs=[whole, whole, whole, half, half],
            out_specs=pl.BlockSpec((1, rows, cols), lambda slot, block, at: (slot, block, 0)),
        ),
        out_shape=jax.ShapeDtypeStruct((slots, 4 * rows, cols), own.dtype),
        compiler_params=pltpu.CompilerParams(vmem_limit_bytes=40 * 2**20),
        cost_estimate=pl.CostEstimate(
            flops=0, bytes_accessed=16 * slots * rows * cols, transcendentals=0
        ),
        name="assemble_weights",
    )(position, own, inner, outer, far_low, far_high)


def factor_kernel(gram_ref, factor_ref):
    def times(left, right):
        return lax.dot_general(
            left, right, (((1,), (0,)), ((), ())), precision=highest, preferred_element_type=f32
        )

    blocks = gram_ref.shape[0]
    row = lax.broadcasted_iota(jnp.int32, (MB, MB), 0)
    col = lax.broadcasted_iota(jnp.int32, (MB, MB), 1)
    eye = jnp.where(row == col, 1.0, 0.0).astype(f32)
    grams, factors = [], []
    for at in range(blocks):
        gram = gram_ref[at]
        trace = jnp.sum(jnp.sum(gram * eye, axis=1, keepdims=True), axis=0, keepdims=True)
        inverse = 1.0 / (jnp.sqrt(trace) + 1e-07)
        grams.append(gram * (inverse * inverse))
        factors.append(inverse)
    for step in range(NS):
        polys = [
            coef_one * eye + coef_two * gram + coef_three * times(gram, gram) for gram in grams
        ]
        if step == 0:
            factors = [poly * factor for poly, factor in zip(polys, factors)]
        else:
            factors = [times(factor, poly) for poly, factor in zip(polys, factors)]
        if step < NS - 1:
            grams = [times(gram, poly) for poly, gram in zip(polys, grams)]
            grams = [times(gram, poly) for poly, gram in zip(polys, grams)]
    for at in range(blocks):
        factor_ref[at] = factors[at]


def muon_factor(gram):
    count = gram.shape[0]
    step = next(size for size in (4, 2, 1) if count % size == 0)
    spec = pl.BlockSpec((step, MB, MB), lambda at: (at, 0, 0))
    return pl.pallas_call(
        factor_kernel,
        grid=(count // step,),
        in_specs=[spec],
        out_specs=spec,
        out_shape=jax.ShapeDtypeStruct(gram.shape, f32),
        compiler_params=pltpu.CompilerParams(vmem_limit_bytes=16 * 2**20),
        cost_estimate=pl.CostEstimate(
            flops=6 * 34 * count * MB**3, bytes_accessed=8 * count * MB**2, transcendentals=0
        ),
        name="muon_factor",
    )(gram)


def solution(mesh):
    n_dp, n_mp = mesh.shape["dp"], mesh.shape["mp"]

    def program(tokens, memory, mem_lengths, *rest):
        group_seqs = mem_lengths.shape[0] // n_dp
        team = n_mp // group_seqs
        paired = team == 2 and n_dp % 2 == 0
        row_count = n_dp // 2 if paired else n_dp
        row_axes = tuple(f"r{at}" for at in range(row_count.bit_length() - 1))
        pair_axes = ("c",) if paired else ()
        names = row_axes + pair_axes + ("s", "t")
        sizes = (2,) * (len(names) - 2) + (group_seqs, team)
        fine = Mesh(mesh.devices.reshape(sizes), names)
        row_spec, col_spec = row_axes + pair_axes, ("s", "t")
        tok_spec = P(names, None)
        mat_spec = P(None, row_spec, col_spec)
        body = functools.partial(on_device, row_axes, paired, group_seqs, team)
        return jax.shard_map(
            body,
            mesh=fine,
            in_specs=(tok_spec, tok_spec, P(row_spec), tok_spec)
            + (mat_spec,) * 4 + (P(),) * 3,
            out_specs=(tok_spec,) * 3 + (mat_spec,) * 4 + (P(),) * 4,
            check_vma=False,
        )(tokens, memory, mem_lengths, *rest)

    return program


def on_device(
    row_axes,
    paired,
    group_seqs,
    team,
    tokens,
    memory,
    mem_lengths,
    cotangent,
    attn_weights,
    ffn_weights,
    attn_momentum,
    ffn_momentum,
    norm_params,
    norm_first,
    norm_second,
):
    team_axis = "c" if paired else "t"
    col_axes = ("s", "t") if paired else ("s",)
    me = lax.axis_index(team_axis)
    row_total = 2 ** len(row_axes)
    col_total = group_seqs * (team if paired else 1)
    both_ways = [(0, 1), (1, 0)]

    def after(value, *others):
        return lax.optimization_barrier((value,) + others)[0]

    def place(value):
        if not paired:
            return value
        moved = lax.ppermute(value, ("c", "t"), [(1, 2), (2, 1)])
        return jnp.where(me == lax.axis_index("t"), value, moved)

    def team_gather(rows):
        if team == 2:
            other = lax.ppermute(rows, team_axis, both_ways)
            return jnp.concatenate([rows, other], axis=0)
        return lax.all_gather(rows, team_axis, axis=0, tiled=True)

    def team_scatter(product, rows):
        if team == 2:
            count = rows[0].shape[-2] // 2
            away = product(*[piece[..., count:, :] for piece in rows]).astype(bf16)
            arrived = lax.ppermute(away, team_axis, both_ways)
            return product(*[piece[..., :count, :] for piece in rows]) + arrived.astype(f32)
        return lax.psum_scatter(product(*rows), team_axis, scatter_dimension=0, tiled=True)

    def in_order(own, other, axis):
        first = jnp.where(me == 0, own, other)
        second = jnp.where(me == 0, other, own)
        return jnp.concatenate([first, second], axis=axis)

    def to_team(value):
        if not paired:
            return value
        cols = value.shape[2] // 2
        away = lax.dynamic_slice_in_dim(value, (1 - me) * cols, cols, 2)
        own = lax.dynamic_slice_in_dim(value, me * cols, cols, 2)
        return in_order(own, lax.ppermute(away, "c", both_ways), 1)

    def from_team(value):
        if not paired:
            return value
        rows = value.shape[1] // 2
        away = lax.dynamic_slice_in_dim(value, (1 - me) * rows, rows, 1)
        own = lax.dynamic_slice_in_dim(value, me * rows, rows, 1)
        return in_order(own, lax.ppermute(away, "c", both_ways), 2)

    def around(value, hop):
        pairs = [(at, (at + hop) % col_total) for at in range(col_total)]
        return lax.ppermute(value, col_axes, pairs)

    def gather_cols(shard):
        return jnp.concatenate([shard] + [around(shard, hop) for hop in range(1, col_total)], axis=2)

    def gather_rows(wide):
        slots, rows, cols = wide.shape
        if len(row_axes) != 2:
            full = lax.all_gather(wide, row_axes, axis=0, tiled=False)
            full = full.transpose(1, 0, 2, 3).reshape(slots, row_total * rows, cols)
            return full, full
        half = rows // 2
        by_outer = lax.ppermute(wide, row_axes[0], both_ways)
        by_inner = lax.ppermute(wide, row_axes[1], both_ways)
        far_low = lax.ppermute(by_outer[:, :half], row_axes[1], both_ways)
        far_high = lax.ppermute(by_inner[:, half:], row_axes[0], both_ways)
        position = lax.axis_index(row_axes).astype(jnp.int32)[None]
        full = assemble(position, wide, by_inner, by_outer, far_low, far_high)
        return full, far_high

    def split_features(rows, axis, other):
        pieces = 2 ** row_axes.index(axis)
        width = rows.shape[1] // (2 * pieces)
        here = lax.axis_index(axis)
        side = 1 - here if other else here
        cuts = [
            lax.dynamic_slice_in_dim(rows, (2 * piece + side) * width, width, 1)
            for piece in range(pieces)
        ]
        return cuts[0] if pieces == 1 else jnp.concatenate(cuts, axis=1)

    def grad_product(rows, grads):
        if grads.ndim == 2:
            grads = grads[None]
        return jnp.einsum("td,ktc->kdc", rows, grads, preferred_element_type=f32)

    def start_grad(rows, grads, axis):
        away = grad_product(split_features(rows, axis, True), grads).astype(bf16)
        return lax.ppermute(away, axis, both_ways)

    def finish_grad(arrived, rows, grads, order, *others):
        if others:
            arrived = after(arrived, *others)
        own = grad_product(split_features(rows, order[0], False), grads)
        piece = (own + arrived.astype(f32)).astype(bf16)
        left = [axis for axis in row_axes if axis != order[0]]
        slots, _, cols = piece.shape
        piece = piece.reshape((slots,) + (2,) * len(left) + (-1, cols))
        for axis in order[1:]:
            at = 1 + left.index(axis)
            here = lax.axis_index(axis)
            away = lax.dynamic_index_in_dim(piece, 1 - here, at, keepdims=False)
            own = lax.dynamic_index_in_dim(piece, here, at, keepdims=False)
            arrived = lax.ppermute(away, axis, both_ways)
            piece = (own.astype(f32) + arrived.astype(f32)).astype(bf16)
            left.remove(axis)
        return piece

    def scatter_cols(pieces, *others):
        if others:
            pieces = list(lax.optimization_barrier(tuple(pieces) + others)[: len(pieces)])
        width = pieces[0].shape[2] // col_total

        def part(hop):
            cut = [piece[:, :, hop * width : (hop + 1) * width] for piece in pieces]
            return jnp.concatenate(cut, axis=0)

        total = part(0).astype(f32)
        for hop in range(1, col_total):
            total = total + around(part(hop), col_total - hop).astype(f32)
        return total

    def muon(momentum, grad, beside):
        slots, rows, cols = momentum.shape
        fresh = 0.5 * momentum + grad
        blocks = fresh.reshape(slots, rows, cols // MB, MB)
        gram = jnp.einsum(
            "sdbi,sdbj->sbij", blocks, blocks, precision=highest, preferred_element_type=f32
        )
        extra = [] if beside is None else [beside]
        sums = jnp.concatenate([gram.reshape(-1, MB)] + extra, axis=0)
        for axis in row_axes:
            sums = sums + lax.ppermute(sums, axis, both_ways)
        count = gram.size // MB
        gram, beside = sums[:count].reshape(gram.shape), sums[count:]
        factor = muon_factor(gram.reshape(-1, MB, MB)).reshape(gram.shape)
        turned = jnp.einsum(
            "sdbi,sbij->sdbj", blocks, factor, precision=highest, preferred_element_type=f32
        )
        return fresh, turned.reshape(slots, rows, cols), beside

    def update(weights, momentum, grad, beside=None):
        fresh, turned, beside = muon(momentum, grad, beside)
        slots = fresh.shape[0]
        both = from_team(jnp.concatenate([fresh, turned], axis=0))
        return both[:slots], weights - step_scale * both[slots:], beside

    step_scale = muon_rate * (attn_weights.shape[1] * row_total * (2 if paired else 1) / MB) ** 0.5
    inner_axis, outer_axis = row_axes[-1], row_axes[0]
    down = row_axes[::-1]
    up = row_axes

    self_mine = to_team(attn_weights[:3].astype(bf16))
    own_tokens = place(tokens)
    self_wide = gather_cols(self_mine)
    own_tokens, rest_src = lax.optimization_barrier((own_tokens, attn_weights[3:]))
    token_rows = team_gather(own_tokens)
    w_qkv, last = gather_rows(self_wide)

    rest_wide = gather_cols(after(to_team(rest_src.astype(bf16)), self_wide))
    own_memory = place(memory)
    lengths = place(mem_lengths)
    length = lax.dynamic_slice_in_dim(lengths, lax.axis_index("s"), 1, 0)
    shift = me * own_tokens.shape[0] if paired else jnp.zeros((), jnp.int32)
    at = jnp.concatenate([length, shift.astype(jnp.int32)[None]])
    w_rest, last = gather_rows(after(rest_wide, last))
    ffn_wide = gather_cols(after(to_team(ffn_weights.astype(bf16)), rest_wide))
    u_both, _ = gather_rows(after(ffn_wide, last))
    u_in, u_out = u_both[0], u_both[1]
    w_so, w_cq = w_rest[0], w_rest[1]
    w_ckv, w_co = w_rest[2:4], w_rest[4]
    own_cotangent = place(after(cotangent, ffn_wide))

    def project(rows, weights):
        return jnp.einsum("td,kdc->ktc", rows, weights, preferred_element_type=f32).astype(bf16)

    def back(rows, weight):
        return jnp.einsum("tc,dc->td", rows, weight, preferred_element_type=f32)

    def back_pair(rows, weights):
        return back(rows[0], weights[0]) + back(rows[1], weights[1])

    def gain(index):
        return norm_params[0, index]

    def bias(index):
        return norm_params[1, index]

    qkv = project(token_rows, w_qkv)
    self_ctx, self_lse = attend_forward((qkv, 0), (qkv, 1), (qkv, 2), at, True)
    self_out = team_scatter(lambda rows: back(rows, w_so), [self_ctx])
    first_out, normed_one, inv_one = norm_forward(
        res_scale * own_tokens.astype(f32) + self_out, gain(0), bias(0)
    )
    first_rows = team_gather(first_out.astype(bf16))
    memory_rows = team_gather(own_memory)
    cross_kv = project(memory_rows, w_ckv)
    cross_q = project(first_rows, w_cq[None])
    cross_ctx, cross_lse = attend_forward((cross_q, 0), (cross_kv, 0), (cross_kv, 1), at, False)
    cross_out = team_scatter(lambda rows: back(rows, w_co), [cross_ctx])
    second, normed_two, inv_two = norm_forward(
        res_scale * first_out + cross_out, gain(1), bias(1)
    )
    second_rows = team_gather(second.astype(bf16))
    hidden = jnp.dot(second_rows, u_in, preferred_element_type=f32)
    active = gelu_exact(hidden).astype(bf16)
    ffn_out = team_scatter(lambda rows: back(rows, u_out), [active])
    mixed_out, normed_three, inv_three = norm_forward(
        res_scale * second + ffn_out, gain(2), bias(2)
    )

    grad_three, gain_three, bias_three = norm_backward(
        own_cotangent.astype(f32), normed_three, inv_three, gain(2)
    )
    grad_ffn_rows = team_gather(grad_three.astype(bf16))
    u_out_way = start_grad(grad_ffn_rows, active, inner_axis)
    grad_active = jnp.dot(grad_ffn_rows, u_out, preferred_element_type=f32)
    grad_hidden = (grad_active * gelu_slope(hidden)).astype(bf16)
    ffn_back = team_scatter(lambda rows: back(rows, u_in), [grad_hidden])
    u_in_way = start_grad(second_rows, grad_hidden, outer_axis)
    grad_second = res_scale * grad_three + ffn_back
    grad_two, gain_two, bias_two = norm_backward(grad_second, normed_two, inv_two, gain(1))
    grad_cross_rows = team_gather(grad_two.astype(bf16))
    grad_cross_ctx = jnp.dot(grad_cross_rows, w_co, preferred_element_type=f32).astype(bf16)
    grad_cq, grad_ckv = attend_backward(
        (cross_q, 0), (cross_kv, 0), (cross_kv, 1), at, cross_ctx, grad_cross_ctx,
        cross_lse, False,
    )
    first_back = team_scatter(lambda rows: back(rows, w_cq), [grad_cq])
    u_out_piece = finish_grad(u_out_way, grad_ffn_rows, active, down, grad_cq)
    u_in_piece = finish_grad(u_in_way, second_rows, grad_hidden, up, grad_cq)
    w7_way = start_grad(after(grad_cross_rows, grad_cq), cross_ctx, inner_axis)
    w4_way = start_grad(first_rows, grad_cq, inner_axis)
    w56_way = start_grad(memory_rows, grad_ckv, outer_axis)
    grad_first = res_scale * grad_two + first_back
    grad_one, gain_one, bias_one = norm_backward(grad_first, normed_one, inv_one, gain(0))
    grad_self_rows = team_gather(grad_one.astype(bf16))
    norm_part = jnp.stack(
        [jnp.stack([gain_one, gain_two, gain_three]), jnp.stack([bias_one, bias_two, bias_three])]
    )
    grad_self_ctx = jnp.dot(grad_self_rows, w_so, preferred_element_type=f32).astype(bf16)
    memory_grad = team_scatter(lambda rows: back_pair(rows, w_ckv), [grad_ckv])
    grad_sq, grad_skv = attend_backward(
        (qkv, 0), (qkv, 1), (qkv, 2), at, self_ctx, grad_self_ctx, self_lse, True
    )
    ffn_grad = scatter_cols([u_in_piece, u_out_piece])
    norm_part = after(norm_part, grad_sq)
    for axis in (("c",) if paired else ()) + ("s", "t"):
        if lax.axis_size(axis) == 2:
            norm_part = norm_part + lax.ppermute(norm_part, axis, both_ways)
        else:
            norm_part = lax.psum(norm_part, axis)
    w3_way = start_grad(grad_self_rows, self_ctx, inner_axis)
    w0_way = start_grad(token_rows, grad_sq, inner_axis)
    w12_way = start_grad(token_rows, grad_skv, outer_axis)
    w7_piece = finish_grad(w7_way, grad_cross_rows, cross_ctx, down, grad_sq)
    w4_piece = finish_grad(w4_way, first_rows, grad_cq, down, grad_sq)
    w56_piece = finish_grad(w56_way, memory_rows, grad_ckv, up, grad_sq)
    token_back = team_scatter(
        lambda q_rows, kv_rows: back(q_rows, w_qkv[0]) + back_pair(kv_rows, w_qkv[1:3]),
        [grad_sq, grad_skv],
    )
    input_grad = res_scale * grad_one + token_back
    w3_piece = finish_grad(w3_way, grad_self_rows, self_ctx, down)
    w0_piece = finish_grad(w0_way, token_rows, grad_sq, down)
    w12_piece = finish_grad(w12_way, token_rows, grad_skv, up)
    cross_grad = scatter_cols([w4_piece, w56_piece, w7_piece])
    self_grad = scatter_cols([w0_piece, w12_piece, w3_piece])

    attn_mom = to_team(attn_momentum)
    ffn_mom = to_team(ffn_momentum)
    ffn_momentum_new, ffn_weights_new, _ = update(ffn_weights, ffn_mom, ffn_grad)
    cross_momentum_new, cross_weights_new, _ = update(attn_weights[4:8], attn_mom[4:8], cross_grad)
    self_momentum_new, self_weights_new, norm_grad = update(
        attn_weights[0:4], attn_mom[0:4], self_grad, norm_part.reshape(-1, MB)
    )
    norm_grad = norm_grad.reshape(norm_params.shape)
    attn_momentum_new = jnp.concatenate([self_momentum_new, cross_momentum_new])
    attn_weights_new = jnp.concatenate([self_weights_new, cross_weights_new])

    norm_first_new = 0.9 * norm_first + 0.1 * norm_grad
    norm_second_new = 0.999 * norm_second + 0.001 * norm_grad * norm_grad
    step_size = (
        norm_first_new
        / (1.0 - 0.9**adam_count)
        / (jnp.sqrt(norm_second_new / (1.0 - 0.999**adam_count)) + 1e-08)
    )
    norm_params_new = norm_params - adam_rate * step_size
    return (
        place(mixed_out),
        place(input_grad),
        place(memory_grad),
        attn_weights_new,
        attn_momentum_new,
        ffn_weights_new,
        ffn_momentum_new,
        norm_grad,
        norm_params_new,
        norm_first_new,
        norm_second_new,
    )
```

time: 2770 us -> 750 us (0.27)
  waiting for transfers between devices: 2090 us -> 254 us
  matrix products: 397 us -> 116 us
  starting transfers between devices: 3.24 us -> 127 us
  Pallas kernels: 0 us -> 107 us
  other arithmetic: 111 us -> 65.4 us
  local copies, waits for them, and re-layouts: 108 us -> 66.8 us
  blocking collectives: 39.7 us -> 0 us
    reduce_scatter x17 -> x0, waiting for transfers between devices: 1250 us -> none  [the longest x5 694 us: scatter_rows(): lax.psum_scatter(partial_value, 'mp', scatter_dimension=0, tiled=True)]
    all_gather x9 -> x0, waiting for transfers between devices: 603 us -> none  [the longest x5 370 us: gather_rows(): return lax.all_gather(rows, 'mp', axis=0, tiled=True)]
    dot_general x88 -> x49, matrix products: 397 us -> 116 us  [the longest x16 40 us: grad_product(): return jnp.einsum('td,ktc->kdc', rows, grads, preferred_element_type=f32)]
    ppermute x0 -> x84, waiting for transfers between devices: none -> 254 us  [the longest x18 97.8 us: around(): return lax.ppermute(value, col_axes, pairs)]
    psum x5 -> x0, waiting for transfers between devices: 237 us -> none  [summed_grams(): return lax.psum((local_gram(attn_blocks), local_gram(ffn_blocks)), 'dp')]
    ppermute x0 -> x84, starting transfers between devices: none -> 127 us  [the longest x7 26.2 us: team_gather(): other = lax.ppermute(rows, team_axis, both_ways)]
    pallas_call x0 -> x10, Pallas kernels: none -> 107 us  [the longest x2 42.1 us: attend_backward(): pl.pallas_call(functools.partial(backward_kernel, causal, chunk), grid_sp...]
    convert_element_type x11 -> x14, other arithmetic: 55.3 us -> 13.3 us  [the longest x8 6.47 us: finish_grad(): piece = (own.astype(f32) + arrived.astype(f32)).astype(bf16)]
  transfers between devices with their start and end apart: 31 -> 84, of which waited for: 27 -> 32; matrix products, arithmetic and copies ran while one was open for 9% -> 30% of each run, Pallas kernels for 0% -> 15%
where the time goes in v1:
time: 750 us; the launch traced here: 740 us
  waiting for transfers between devices  254 us (34%)
  starting transfers between devices  127 us (17%)
  matrix products  116 us (15%)
  Pallas kernels  107 us (14%)
  local copies, waits for them, and re-layouts  66.8 us (9%)
  other arithmetic  65.4 us (9%)
    ppermute x18, waiting for transfers between devices, around(): return lax.ppermute(value, col_axes, pairs)  97.8 us
    ppermute x8, waiting for transfers between devices, finish_grad(): arrived = lax.ppermute(away, axis, both_ways)  54 us
    pallas_call x2, Pallas kernels, attend_backward(): pl.pallas_call(functools.partial(backward_kernel, causal, chunk), grid_sp...  42.1 us
    pallas_call x2, Pallas kernels, attend_forward(): pl.pallas_call(functools.partial(forward_kernel, causal, chunk), grid_spe...  41.7 us
    dot_general x16, matrix products, grad_product(): return jnp.einsum('td,ktc->kdc', rows, grads, preferred_element_type=f32)  40 us
    dot_general x20, matrix products, back(): return jnp.einsum('tc,dc->td', rows, weight, preferred_element_type=f32)  39.4 us
    unnamed x235, local copies, waits for them, and re-layouts  35.1 us
    ppermute x3, waiting for transfers between devices, gather_rows(): by_inner = lax.ppermute(wide, row_axes[1], both_ways)  29.4 us
  transfers between devices with their start and end apart: 84, of which 32 were waited for; matrix products, arithmetic and copies ran while one was open for 30% of the time, Pallas kernels for 15%

profile of v1, /device:TPU:0, one launch (start us, length us, event | category | flops | bytes accessed | tf_op | source)
XLA Modules:
  0.0 739.6 jit_solution(7432919344289378125)
XLA Ops:
  14.4 14.7 %collective-permute-done.5 = bf16[3,256,128]{2,1,0:T(8,128)(2,1)S(1)} collective-permute-done((bf16[3,256,128]{2,1,0:T(8,128)(2,1)S(1)}, bf16[3,256,128]{2,1,0:T(8,128)(2,1)S(1)}, u32[]{:S(2)}, u32[]{:S(2)}) %collective-permute-start.5) | collective-permute-done | bytes 196640 | tf_op jit(solution)/shard_map/ppermute | solution.py:418
  42.1 7.9 %collective-permute-done.6.inner_ref = bf16[3,256,512]{2,1,0:T(8,128)(2,1)S(1)} collective-permute-done((bf16[3,256,512]{2,1,0:T(8,128)(2,1)S(1)}, bf16[3,256,512]{2,1,0:T(8,128)(2,1)S(1)}, u32[]{:S(2)}, u32[]{:S(2)}) %collective-permute-start.6) | collective-permute-done | bytes 786464 | tf_op jit(solution)/shard_map/ppermute | solution.py:431
  57.4 8.5 %collective-permute-done.13 = bf16[5,256,128]{2,1,0:T(8,128)(2,1)} collective-permute-done((bf16[5,256,128]{2,1,0:T(8,128)(2,1)}, bf16[5,256,128]{2,1,0:T(8,128)(2,1)}, u32[]{:S(2)}, u32[]{:S(2)}) %collective-permute-start.13) | collective-permute-done | bytes 327712 | tf_op jit(solution)/shard_map/ppermute | solution.py:418
  84.4 21.6 %collective-permute-done.15.inner_ref = bf16[5,256,512]{2,1,0:T(8,128)(2,1)S(1)} collective-permute-done((bf16[5,256,512]{2,1,0:T(8,128)(2,1)S(1)}, bf16[5,256,512]{2,1,0:T(8,128)(2,1)S(1)}, u32[]{:S(2)}, u32[]{:S(2)}) %collective-permute-start.15) | collective-permute-done | bytes 1310752 | tf_op jit(solution)/shard_map/ppermute | solution.py:431
  107.7 17.1 %attend_forward_causal.1 = (bf16[1024,512]{1,0:T(8,128)(2,1)S(1)}, f32[4,8,1024]{2,1,0:T(8,128)S(1)}) custom-call(s32[2]{0:T(128)S(1)} %pad_add_fusion.at_ref, bf16[3,1024,512]{2,1,0:T(8,128)(2,1)S(1)} %convert_bitcast_fusion.q_ref.k_ref.v_ref, bf16[3,1024,512]{2,1,0:T(8,128)(2,1)S(1)} %convert_bitcast_fusion.q_ref.k_ref.v_ref, ...), custom_call_target="tpu_custom_call" | custom-call | flops 17179869184 | bytes 4194304 | tf_op jit(solution)/shard_map/attend_forward_causal/pallas_call | solution.py:172
  147.7 8.3 %collective-permute-done.26 = bf16[2,256,512]{2,1,0:T(8,128)(2,1)S(1)} collective-permute-done((bf16[2,256,512]{2,1,0:T(8,128)(2,1)S(1)}, bf16[2,256,512]{2,1,0:T(8,128)(2,1)S(1)}, u32[]{:S(2)}, u32[]{:S(2)}) %collective-permute-start.26) | collective-permute-done | bytes 524320 | tf_op jit(solution)/shard_map/ppermute | solution.py:418
  156.1 22.1 %collective-permute-done.27 = bf16[2,256,512]{2,1,0:T(8,128)(2,1)S(1)} collective-permute-done((bf16[2,256,512]{2,1,0:T(8,128)(2,1)S(1)}, bf16[2,256,512]{2,1,0:T(8,128)(2,1)S(1)}, u32[]{:S(2)}, u32[]{:S(2)}) %collective-permute-start.27) | collective-permute-done | bytes 524320 | tf_op jit(solution)/shard_map/ppermute | solution.py:418
  186.1 24.6 %attend_forward_cross.1 = (bf16[1024,512]{1,0:T(8,128)(2,1)S(1)}, f32[4,8,1024]{2,1,0:T(8,128)S(1)}) custom-call(s32[2]{0:T(128)S(1)} %pad_add_fusion.at_ref, bf16[1,1024,512]{2,1,0:T(8,128)(2,1)S(1)} %fusion.57.q_ref, bf16[2,1024,512]{2,1,0:T(8,128)(2,1)S(1)} %convert_bitcast_fusion.1.k_ref.v_ref, bf16[2,1024,512]{2,1,0:T(8,128)(2,1)S(1)} %convert_bitcast_fusion.1.k_ref.v_ref), custom_call_target="tpu_custom_call" | custom-call | flops 17179869184 | bytes 4194304 | tf_op jit(solution)/shard_map/attend_forward_cross/pallas_call | solution.py:172
  211.6 15.5 %collective-permute-done.30.outer_ref = bf16[2,256,2048]{2,1,0:T(8,128)(2,1)S(1)} collective-permute-done((bf16[2,256,2048]{2,1,0:T(8,128)(2,1)S(1)}, bf16[2,256,2048]{2,1,0:T(8,128)(2,1)S(1)}, u32[]{:S(2)}, u32[]{:S(2)}) %collective-permute-start.30) | collective-permute-done | bytes 2097184 | tf_op jit(solution)/shard_map/ppermute | solution.py:430
  231.5 19.7 %collective-permute-done.31.far_low_ref = bf16[2,128,2048]{2,1,0:T(8,128)(2,1)S(1)} collective-permute-done((bf16[2,128,2048]{2,1,0:T(8,128)(2,1)S(1)}, bf16[2,128,2048]{2,1,0:T(8,128)(2,1)S(1)}, u32[]{:S(2)}, u32[]{:S(2)}) %collective-permute-start.31) | collective-permute-done | bytes 1048608 | tf_op jit(solution)/shard_map/ppermute | solution.py:432
  256.3 9.3 %multiply_convert_fusion = (bf16[1024,2048]{1,0:T(8,128)(2,1)S(1)}, f32[1024,2048]{1,0:T(8,128)}) fusion(bf16[2,1024,2048]{2,1,0:T(8,128)(2,1)} %assemble_weights.5, bf16[512,1024]{1,0:T(8,128)(2,1)S(1)} %collective-permute-done.24, bf16[512,1024]{1,0:T(8,128)(2,1)S(1)} %fusion.42), kind=kOutput, calls=%fused_computation.7 | convolution fusion | flops 4309647360 | bytes 18874368 | tf_op jit(solution)/shard_map/dot_general | solution.py:572
  277.6 20.5 %collective-permute-start.36 = (bf16[512,1024]{1,0:T(8,128)(2,1)}, bf16[512,1024]{1,0:T(8,128)(2,1)}, u32[]{:S(2)}, u32[]{:S(2)}) collective-permute-start(bf16[512,1024]{1,0:T(8,128)(2,1)} %get-tuple-element.99), channel_id=1, source_target_pairs={{0,4},{4,0},{1,5},{5,1},{2,6},{6,2},{3,7},{7,3},{8,12},{12,8},{9,1... | collective-permute-start | bytes 3145736 | tf_op jit(solution)/shard_map/ppermute | solution.py:383
  303.6 10.4 %fusion.5 = bf16[1024,2048]{1,0:T(8,128)(2,1)S(1)} fusion(f32[1024,2048]{1,0:T(8,128)} %get-tuple-element.198, bf16[2,1024,2048]{2,1,0:T(8,128)(2,1)} %assemble_weights.5, bf16[512,1024]{1,0:T(8,128)(2,1)} %collective-permute-done.36, bf16[512,1024]{1,0:T(8,128)(2,1)} %get-tuple-element.99), kind=kOutput, calls=%fused_computation.6 | convolution fusion | flops 4320133120 | bytes 18874368 | tf_op jit(solution)/shard_map/dot_general | solution.py:584
  314.0 7.2 fusion.52
  365.7 24.7 %attend_backward_cross.1 = (bf16[1024,512]{1,0:T(8,128)(2,1)S(1)}, bf16[2,1024,512]{2,1,0:T(8,128)(2,1)}) custom-call(s32[2]{0:T(128)S(1)} %pad_add_fusion.at_ref, bf16[1,1024,512]{2,1,0:T(8,128)(2,1)S(1)} %copy-done.12, bf16[2,1024,512]{2,1,0:T(8,128)(2,1)} %copy-done.9, bf16[2,1024,512]{2,1,0:T(8,128)(2,1)} %copy-done.9, bf16[1024,512]{1,0:T(8,128)(2,1)S(1)} %copy-done.8, ...), custom_call_target="tpu_custom_call" | custom-call | flops 21474836480 | bytes 8388608 | tf_op jit(solution)/shard_map/attend_backward_cross/pallas_call | solution.py:205
  422.6 14.0 %collective-permute-done.77 = bf16[1,256,2048]{2,1,0:T(8,128)(2,1)S(1)} collective-permute-done((bf16[1,256,2048]{2,1,0:T(8,128)(2,1)S(1)}, bf16[1,256,2048]{2,1,0:T(8,128)(2,1)S(1)}, u32[]{:S(2)}, u32[]{:S(2)}) %collective-permute-start.77) | collective-permute-done | bytes 1048608 | tf_op jit(solution)/shard_map/ppermute | solution.py:471
  450.8 8.9 %collective-permute-done.80 = bf16[2,256,512]{2,1,0:T(8,128)(2,1)S(1)} collective-permute-done((bf16[2,256,512]{2,1,0:T(8,128)(2,1)S(1)}, bf16[2,256,512]{2,1,0:T(8,128)(2,1)S(1)}, u32[]{:S(2)}, u32[]{:S(2)}) %collective-permute-start.80) | collective-permute-done | bytes 524320 | tf_op jit(solution)/shard_map/ppermute | solution.py:418
  461.0 19.0 %collective-permute-done.79 = bf16[2,256,512]{2,1,0:T(8,128)(2,1)S(1)} collective-permute-done((bf16[2,256,512]{2,1,0:T(8,128)(2,1)S(1)}, bf16[2,256,512]{2,1,0:T(8,128)(2,1)S(1)}, u32[]{:S(2)}, u32[]{:S(2)}) %collective-permute-start.79) | collective-permute-done | bytes 524320 | tf_op jit(solution)/shard_map/ppermute | solution.py:418
  489.4 17.5 %attend_backward_causal.1 = (bf16[1024,512]{1,0:T(8,128)(2,1)S(1)}, bf16[2,1024,512]{2,1,0:T(8,128)(2,1)S(1)}) custom-call(s32[2]{0:T(128)S(1)} %pad_add_fusion.at_ref, bf16[3,1024,512]{2,1,0:T(8,128)(2,1)} %copy-done.10, bf16[3,1024,512]{2,1,0:T(8,128)(2,1)} %copy-done.10, bf16[3,1024,512]{2,1,0:T(8,128)(2,1)} %copy-done.10, ...), custom_call_target="tpu_custom_call" | custom-call | flops 21474836480 | bytes 8388608 | tf_op jit(solution)/shard_map/attend_backward_causal/pallas_call | solution.py:205
  514.4 10.1 %collective-permute-start.41 = (bf16[512,1024]{1,0:T(8,128)(2,1)}, bf16[512,1024]{1,0:T(8,128)(2,1)}, u32[]{:S(2)}, u32[]{:S(2)}) collective-permute-start(bf16[512,1024]{1,0:T(8,128)(2,1)} %add_convert_fusion.1), channel_id=1, source_target_pairs={{0,4},{4,0},{1,5},{5,1},{2,6},{6,2},{3,7},{7,3},{8,12},{12,8},{9,1... | collective-permute-start | bytes 3145736 | tf_op jit(solution)/shard_map/ppermute | solution.py:391
  567.3 24.5 %collective-permute-done.62 = bf16[1,256,512]{1,2,0:T(8,128)(2,1)S(1)} collective-permute-done((bf16[1,256,512]{1,2,0:T(8,128)(2,1)}, bf16[1,256,512]{1,2,0:T(8,128)(2,1)S(1)}, u32[]{:S(2)}, u32[]{:S(2)}) %collective-permute-start.62) | collective-permute-done | bytes 262176 | tf_op jit(solution)/shard_map/ppermute | solution.py:471
  599.1 7.8 %collective-permute-done.46 = bf16[1,512,512]{2,1,0:T(8,128)(2,1)} collective-permute-done((bf16[1,512,512]{2,1,0:T(8,128)(2,1)}, bf16[1,512,512]{2,1,0:T(8,128)(2,1)}, u32[]{:S(2)}, u32[]{:S(2)}) %collective-permute-start.46) | collective-permute-done | bytes 524320 | tf_op jit(solution)/shard_map/ppermute | solution.py:456
  629.1 8.7 %muon_factor.5 = f32[8,128,128]{2,1,0:T(8,128)S(1)} custom-call(f32[8,128,128]{2,1,0:T(8,128)S(1)} %bitcast.321), custom_call_target="tpu_custom_call" | custom-call | flops 3422552064 | bytes 1048576 | tf_op jit(solution)/shard_map/muon_factor/pallas_call | solution.py:305
  681.4 9.6 %collective-permute-done.53 = bf16[4,256,128]{1,2,0:T(8,128)(2,1)S(1)} collective-permute-done((bf16[4,256,128]{1,2,0:T(8,128)(2,1)S(1)}, bf16[4,256,128]{1,2,0:T(8,128)(2,1)S(1)}, u32[]{:S(2)}, u32[]{:S(2)}) %collective-permute-start.53) | collective-permute-done | bytes 262176 | tf_op jit(solution)/shard_map/ppermute | solution.py:418
  (575 shorter events, 384.8 us)
Async XLA Ops:
  0.6 35.8 %collective-permute-start = (bf16[512,1024]{1,0:T(8,128)(2,1)}, bf16[512,1024]{1,0:T(8,128)(2,1)}, u32[]{:S(2)}, u32[]{:S(2)}) collective-permute-start(bf16[512,1024]{1,0:T(8,128)(2,1)} %param.11), channel_id=1, source_target_pairs={{1,4},{4,1},{3,6},{6,3},{9,12},{12,9},{11,14},{14,11},{17,20},{20,... | collective-permute-start | bytes 3145736 | tf_op jit(solution)/shard_map/ppermute | solution.py:378
  39.9 38.6 %collective-permute-start.10 = (bf16[512,1024]{1,0:T(8,128)(2,1)}, bf16[512,1024]{1,0:T(8,128)(2,1)}, u32[]{:S(2)}, u32[]{:S(2)}) collective-permute-start(bf16[512,1024]{1,0:T(8,128)(2,1)} %broadcast_select_fusion.5), channel_id=1, source_target_pairs={{0,4},{4,0},{1,5},{5,1},{2,6},{6,2},{3,7},{7,3},{8,12},{12,8},{9,1... | collective-permute-start | bytes 3145736 | tf_op jit(solution)/shard_map/ppermute | solution.py:383
  65.9 69.7 %collective-permute-start.21 = (bf16[512,1024]{1,0:T(8,128)(2,1)S(1)}, bf16[512,1024]{1,0:T(8,128)(2,1)}, u32[]{:S(2)}, u32[]{:S(2)}) collective-permute-start(bf16[512,1024]{1,0:T(8,128)(2,1)S(1)} %copy-done.51), channel_id=1, source_target_pairs={{1,4},{4,1},{3,6},{6,3},{9,12},{12,9},{11,14},{14,11},{17,20},{20,... | collective-permute-start | bytes 3145736 | tf_op jit(solution)/shard_map/ppermute | solution.py:378
  69.7 36.3 %collective-permute-start.15 = (bf16[5,256,512]{2,1,0:T(8,128)(2,1)S(1)}, bf16[5,256,512]{2,1,0:T(8,128)(2,1)S(1)}, u32[]{:S(2)}, u32[]{:S(2)}) collective-permute-start(bf16[5,256,512]{2,1,0:T(8,128)(2,1)S(1)} %constant_dynamic-update-slice_fusion.2.own_ref), channel_id=1, source_target_pairs={{0,8},{8,0},{1,9},{9,1},{2,10},{10,2},{3,11},{11,3},{4,12},{12,4},... | collective-permute-start | bytes 3932168 | tf_op jit(solution)/shard_map/ppermute | solution.py:431
  70.9 35.8 %collective-permute-start.16 = (bf16[5,256,512]{2,1,0:T(8,128)(2,1)S(1)}, bf16[5,256,512]{2,1,0:T(8,128)(2,1)S(1)}, u32[]{:S(2)}, u32[]{:S(2)}) collective-permute-start(bf16[5,256,512]{2,1,0:T(8,128)(2,1)S(1)} %constant_dynamic-update-slice_fusion.2.own_ref), channel_id=1, source_target_pairs={{0,16},{16,0},{1,17},{17,1},{2,18},{18,2},{3,19},{19,3},{4,20},{20... | collective-permute-start | bytes 3932168 | tf_op jit(solution)/shard_map/ppermute | solution.py:430
  135.7 45.7 %collective-permute-start.22 = (bf16[512,1024]{1,0:T(8,128)(2,1)S(1)}, bf16[512,1024]{1,0:T(8,128)(2,1)S(1)}, u32[]{:S(2)}, u32[]{:S(2)}) collective-permute-start(bf16[512,1024]{1,0:T(8,128)(2,1)S(1)} %broadcast_select_fusion.4), channel_id=1, source_target_pairs={{0,4},{4,0},{1,5},{5,1},{2,6},{6,2},{3,7},{7,3},{8,12},{12,8},{9,1... | collective-permute-start | bytes 3145736 | tf_op jit(solution)/shard_map/ppermute | solution.py:383
  141.0 37.2 %collective-permute-start.27 = (bf16[2,256,512]{2,1,0:T(8,128)(2,1)S(1)}, bf16[2,256,512]{2,1,0:T(8,128)(2,1)S(1)}, u32[]{:S(2)}, u32[]{:S(2)}) collective-permute-start(bf16[2,256,512]{2,1,0:T(8,128)(2,1)S(1)} %pad_maximum_fusion.21), channel_id=1, source_target_pairs={{0,2},{1,3},{2,0},{3,1},{4,6},{5,7},{6,4},{7,5},{8,10},{9,11},{10,... | collective-permute-start | bytes 1572872 | tf_op jit(solution)/shard_map/ppermute | solution.py:418
  147.6 36.2 %collective-permute-start.20 = (bf16[512,1024]{1,0:T(8,128)(2,1)S(1)}, bf16[512,1024]{1,0:T(8,128)(2,1)S(1)}, u32[]{:S(2)}, u32[]{:S(2)}) collective-permute-start(bf16[512,1024]{1,0:T(8,128)(2,1)S(1)} %fusion.41), channel_id=1, source_target_pairs={{0,4},{4,0},{1,5},{5,1},{2,6},{6,2},{3,7},{7,3},{8,12},{12,8},{9,1... | collective-permute-start | bytes 3145736 | tf_op jit(solution)/shard_map/ppermute | solution.py:383
  178.3 49.5 %collective-permute-start.29 = (bf16[2,256,2048]{2,1,0:T(8,128)(2,1)S(1)}, bf16[2,256,2048]{2,1,0:T(8,128)(2,1)S(1)}, u32[]{:S(2)}, u32[]{:S(2)}) collective-permute-start(bf16[2,256,2048]{2,1,0:T(8,128)(2,1)S(1)} %constant_dynamic-update-slice_fusion.6.own_ref), channel_id=1, source_target_pairs={{0,8},{8,0},{1,9},{9,1},{2,10},{10,2},{3,11},{11,3},{4,12},{12,4},... | collective-permute-start | bytes 6291464 | tf_op jit(solution)/shard_map/ppermute | solution.py:431
  179.9 47.2 %collective-permute-start.30 = (bf16[2,256,2048]{2,1,0:T(8,128)(2,1)S(1)}, bf16[2,256,2048]{2,1,0:T(8,128)(2,1)S(1)}, u32[]{:S(2)}, u32[]{:S(2)}) collective-permute-start(bf16[2,256,2048]{2,1,0:T(8,128)(2,1)S(1)} %constant_dynamic-update-slice_fusion.6.own_ref), channel_id=1, source_target_pairs={{0,16},{16,0},{1,17},{17,1},{2,18},{18,2},{3,19},{19,3},{4,20},{20... | collective-permute-start | bytes 6291464 | tf_op jit(solution)/shard_map/ppermute | solution.py:430
  355.6 50.8 %collective-permute-start.76 = (bf16[1,512,2048]{2,1,0:T(8,128)(2,1)}, bf16[1,512,2048]{2,1,0:T(8,128)(2,1)}, u32[]{:S(2)}, u32[]{:S(2)}) collective-permute-start(bf16[1,512,2048]{2,1,0:T(8,128)(2,1)} %fusion.17), channel_id=1, source_target_pairs={{0,8},{8,0},{1,9},{9,1},{2,10},{10,2},{3,11},{11,3},{4,12},{12,4},... | collective-permute-start | bytes 6291464 | tf_op jit(solution)/shard_map/ppermute | solution.py:456
  360.9 52.1 %collective-permute-start.74 = (bf16[1,512,2048]{2,1,0:T(8,128)(2,1)}, bf16[1,512,2048]{2,1,0:T(8,128)(2,1)}, u32[]{:S(2)}, u32[]{:S(2)}) collective-permute-start(bf16[1,512,2048]{2,1,0:T(8,128)(2,1)} %fusion.16), channel_id=1, source_target_pairs={{0,16},{16,0},{1,17},{17,1},{2,18},{18,2},{3,19},{19,3},{4,20},{20... | collective-permute-start | bytes 6291464 | tf_op jit(solution)/shard_map/ppermute | solution.py:456
  396.4 50.9 %collective-permute-start.43 = (bf16[512,1024]{1,0:T(8,128)(2,1)S(1)}, bf16[512,1024]{1,0:T(8,128)(2,1)S(1)}, u32[]{:S(2)}, u32[]{:S(2)}) collective-permute-start(bf16[512,1024]{1,0:T(8,128)(2,1)S(1)} %add_convert_fusion), channel_id=1, source_target_pairs={{0,4},{4,0},{1,5},{5,1},{2,6},{6,2},{3,7},{7,3},{8,12},{12,8},{9,1... | collective-permute-start | bytes 3145736 | tf_op jit(solution)/shard_map/ppermute | solution.py:391
  422.6 63.9 %collective-permute-start.40 = (bf16[512,1024]{1,0:T(8,128)(2,1)S(1)}, bf16[512,1024]{1,0:T(8,128)(2,1)S(1)}, u32[]{:S(2)}, u32[]{:S(2)}) collective-permute-start(bf16[512,1024]{1,0:T(8,128)(2,1)S(1)} %get-tuple-element.92), channel_id=1, source_target_pairs={{0,4},{4,0},{1,5},{5,1},{2,6},{6,2},{3,7},{7,3},{8,12},{12,8},{9,1... | collective-permute-start | bytes 3145736 | tf_op jit(solution)/shard_map/ppermute | solution.py:383
  444.8 36.6 %collective-permute-start.78 = (bf16[2,256,512]{2,1,0:T(8,128)(2,1)S(1)}, bf16[2,256,512]{2,1,0:T(8,128)(2,1)S(1)}, u32[]{:S(2)}, u32[]{:S(2)}) collective-permute-start(bf16[2,256,512]{2,1,0:T(8,128)(2,1)S(1)} %pad_maximum_fusion.22), channel_id=1, source_target_pairs={{0,3},{1,0},{2,1},{3,2},{4,7},{5,4},{6,5},{7,6},{8,11},{9,8},{10,9... | collective-permute-start | bytes 1572872 | tf_op jit(solution)/shard_map/ppermute | solution.py:418
  447.3 84.7 %collective-permute-start.65 = (bf16[1,512,512]{2,1,0:T(8,128)(2,1)}, bf16[1,512,512]{2,1,0:T(8,128)(2,1)}, u32[]{:S(2)}, u32[]{:S(2)}) collective-permute-start(bf16[1,512,512]{2,1,0:T(8,128)(2,1)} %fusion.69), channel_id=1, source_target_pairs={{0,8},{8,0},{1,9},{9,1},{2,10},{10,2},{3,11},{11,3},{4,12},{12,4},... | collective-permute-start | bytes 1572872 | tf_op jit(solution)/shard_map/ppermute | solution.py:456
  459.7 54.7 %collective-permute-start.63 = (bf16[2,512,512]{2,1,0:T(8,128)(2,1)}, bf16[2,512,512]{2,1,0:T(8,128)(2,1)}, u32[]{:S(2)}, u32[]{:S(2)}) collective-permute-start(bf16[2,512,512]{2,1,0:T(8,128)(2,1)} %fusion.56), channel_id=1, source_target_pairs={{0,16},{16,0},{1,17},{17,1},{2,18},{18,2},{3,19},{19,3},{4,20},{20... | collective-permute-start | bytes 3145736 | tf_op jit(solution)/shard_map/ppermute | solution.py:456
  480.0 56.7 %collective-permute-start.61 = (bf16[1,512,512]{2,1,0:T(8,128)(2,1)}, bf16[1,512,512]{2,1,0:T(8,128)(2,1)}, u32[]{:S(2)}, u32[]{:S(2)}) collective-permute-start(bf16[1,512,512]{2,1,0:T(8,128)(2,1)} %fusion.68), channel_id=1, source_target_pairs={{0,8},{8,0},{1,9},{9,1},{2,10},{10,2},{3,11},{11,3},{4,12},{12,4},... | collective-permute-start | bytes 1572872 | tf_op jit(solution)/shard_map/ppermute | solution.py:456
  481.4 176.1 %collective-permute-start.44 = (f32[512,1024]{1,0:T(8,128)}, f32[512,1024]{1,0:T(8,128)}, u32[]{:S(2)}, u32[]{:S(2)}) collective-permute-start(f32[512,1024]{1,0:T(8,128)} %convert_add_fusion.2), channel_id=1, source_target_pairs={{1,4},{4,1},{3,6},{6,3},{9,12},{12,9},{11,14},{14,11},{17,20},{20,... | collective-permute-start | bytes 6291464 | tf_op jit(solution)/shard_map/ppermute | solution.py:378
  486.5 69.7 %collective-permute-start.81 = (f32[1024,128]{1,0:T(8,128)}, f32[1024,128]{1,0:T(8,128)}, u32[]{:S(2)}, u32[]{:S(2)}) collective-permute-start(f32[1024,128]{1,0:T(8,128)} %bitcast.107), channel_id=1, source_target_pairs={{0,16},{16,0},{1,17},{17,1},{2,18},{18,2},{3,19},{19,3},{4,20},{20... | collective-permute-start | bytes 1572872 | tf_op jit(solution)/shard_map/ppermute | solution.py:500
  514.4 148.2 %collective-permute-start.41 = (bf16[512,1024]{1,0:T(8,128)(2,1)}, bf16[512,1024]{1,0:T(8,128)(2,1)}, u32[]{:S(2)}, u32[]{:S(2)}) collective-permute-start(bf16[512,1024]{1,0:T(8,128)(2,1)} %add_convert_fusion.1), channel_id=1, source_target_pairs={{0,4},{4,0},{1,5},{5,1},{2,6},{6,2},{3,7},{7,3},{8,12},{12,8},{9,1... | collective-permute-start | bytes 3145736 | tf_op jit(solution)/shard_map/ppermute | solution.py:391
  531.9 61.5 %collective-permute-start.50 = (bf16[1,512,512]{2,1,0:T(8,128)(2,1)}, bf16[1,512,512]{2,1,0:T(8,128)(2,1)}, u32[]{:S(2)}, u32[]{:S(2)}) collective-permute-start(bf16[1,512,512]{2,1,0:T(8,128)(2,1)} %fusion.67), channel_id=1, source_target_pairs={{0,8},{8,0},{1,9},{9,1},{2,10},{10,2},{3,11},{11,3},{4,12},{12,4},... | collective-permute-start | bytes 1572872 | tf_op jit(solution)/shard_map/ppermute | solution.py:456
  560.1 89.5 %collective-permute-start.48 = (bf16[2,512,512]{2,1,0:T(8,128)(2,1)}, bf16[2,512,512]{2,1,0:T(8,128)(2,1)}, u32[]{:S(2)}, u32[]{:S(2)}) collective-permute-start(bf16[2,512,512]{2,1,0:T(8,128)(2,1)} %fusion.55), channel_id=1, source_target_pairs={{0,16},{16,0},{1,17},{17,1},{2,18},{18,2},{3,19},{19,3},{4,20},{20... | collective-permute-start | bytes 3145736 | tf_op jit(solution)/shard_map/ppermute | solution.py:456
  676.6 59.4 %collective-permute-start.42 = (f32[512,1024]{1,0:T(8,128)}, f32[512,1024]{1,0:T(8,128)}, u32[]{:S(2)}, u32[]{:S(2)}) collective-permute-start(f32[512,1024]{1,0:T(8,128)} %add_add_fusion), channel_id=1, source_target_pairs={{1,4},{4,1},{3,6},{6,3},{9,12},{12,9},{11,14},{14,11},{17,20},{20,... | collective-permute-start | bytes 6291464 | tf_op jit(solution)/shard_map/ppermute | solution.py:378
  (166 other events, 2163.1 us)
